TPU v7x, 32 devices: a whole 2x2x4 slice. The times are simulated.
32 devices in a mesh: clique: 2 (over core), dp: 4 (over z), hst: 4 (over y, x).
Axes of the slice: x: 2, y: 2, z: 4, core: 2. Of those that a mesh axis runs over, the one named last changes fastest.
Arguments:
- hot_table: bfloat16 [4096, 1024], P('clique'), may hold values from -6 to 6
- cold_table: bfloat16 [8192, 1024], P('hst'), may hold values from -6 to 6
- seed_source: int32 [32, 64], P(('clique', 'dp', 'hst')), may hold values from 0 to 5119, as said below
- hop1_source: int32 [32, 640], P(('clique', 'dp', 'hst')), may hold values from 0 to 5119, as said below
- hop2_source: int32 [32, 9600], P(('clique', 'dp', 'hst')), may hold values from 0 to 5119, as said below
- cold_ask: int32 [32, 4, 256], P(('clique', 'dp', 'hst')), may hold values from 0 to 2047, as said below
- cotangent: bfloat16 [2048, 1024], P(('clique', 'dp', 'hst')), may hold values from -0.13183594 to 0.13183594
- w1_self: bfloat16 [1024, 1024], replicated, may hold values from -0.1875 to 0.1875
- w1_neigh: bfloat16 [1024, 1024], replicated, may hold values from -0.1875 to 0.1875
- w2_self: bfloat16 [1024, 1024], replicated, may hold values from -0.1875 to 0.1875
- w2_neigh: bfloat16 [1024, 1024], replicated, may hold values from -0.1875 to 0.1875
Outputs:
- embedding: bfloat16 [2048, 1024], P(('clique', 'dp', 'hst'))
- grad_w1_self: float32 [1024, 1024], P(('clique', 'hst'))
- grad_w1_neigh: float32 [1024, 1024], P(('clique', 'hst'))
- grad_w2_self: float32 [1024, 1024], P(('clique', 'hst'))
- grad_w2_neigh: float32 [1024, 1024], P(('clique', 'hst'))
Inputs may be any that keep to these rules, and one draw needn't show every extreme that they name: `seed_source`: values below 4096 name a hot cache row; a value 4096 + o * 256 + s names slot s of this device's request to cold owner o. Every slot of every owner is named by at least one node of the device's tree (seed, first-hop or second-hop). `hop1_source`: as for seed_source. `hop2_source`: as for seed_source. `cold_ask`: each entry is a row within the owner's block of cold_table.
All inputs are finite; a program needn't handle non-finite values.
Results may differ from a plain program's by a relative error of at most 0.0044.
The roundings to bfloat16 on the way count: a program that leaves them out, or rounds other values in their place, can miss the bound.
Values may be sent and summed in bfloat16 or wider, within the bound.
A program may use at most 128 MiB of HBM per device.

v0:
```python
import jax
import jax.numpy as jnp
from jax import lax
from jax.sharding import PartitionSpec as P

K2 = 10
K1 = 15


def mean_rows(values, fanout):
    groups = values.shape[0] // fanout
    total = jnp.sum(values.reshape(groups, fanout, values.shape[1]), axis=1, dtype=jnp.float32)
    return (total / fanout).astype(jnp.bfloat16)


def matmul(left, right):
    return jnp.dot(left, right, preferred_element_type=jnp.float32)


def inner_rows(left, right):
    return lax.dot_general(
        left, right, (((0,), (0,)), ((), ())), preferred_element_type=jnp.float32
    )


def inner_cols(left, right):
    return lax.dot_general(
        left, right, (((1,), (1,)), ((), ())), preferred_element_type=jnp.float32
    )


def body(
    hot_table,
    cold_table,
    seed_source,
    hop1_source,
    hop2_source,
    cold_ask,
    cotangent,
    w1_self,
    w1_neigh,
    w2_self,
    w2_neigh,
):
    width = hot_table.shape[1]
    hidden_width = w1_self.shape[1]
    seeds_count = seed_source.shape[1]
    hot_full = lax.all_gather(hot_table, "clique", axis=0, tiled=True)
    picked = jnp.take(
        cold_table,
        lax.all_to_all(cold_ask[0], "hst", split_axis=0, concat_axis=0, tiled=True),
        axis=0,
    )
    cold_rows = lax.all_to_all(picked, "hst", split_axis=0, concat_axis=0, tiled=True)
    lookup = jnp.concatenate([hot_full, cold_rows.reshape(-1, width)], 0)
    seed_feat = jnp.take(lookup, seed_source[0], axis=0)
    hop1_feat = jnp.take(lookup, hop1_source[0], axis=0)
    hop2_feat = jnp.take(lookup, hop2_source[0], axis=0)
    level_in = jnp.concatenate([seed_feat, hop1_feat], 0)
    level_mean = jnp.concatenate([mean_rows(hop1_feat, K2), mean_rows(hop2_feat, K1)], 0)
    pre = matmul(level_in, w1_self) + matmul(level_mean, w1_neigh)
    hidden = jnp.maximum(pre, 0.0).astype(jnp.bfloat16)
    hidden_seed = hidden[:seeds_count]
    hidden_mean = mean_rows(hidden[seeds_count:], K2)
    embedding = (matmul(hidden_seed, w2_self) + matmul(hidden_mean, w2_neigh)).astype(jnp.bfloat16)
    grad_seed = inner_cols(cotangent, w2_self)
    grad_mean = inner_cols(cotangent, w2_neigh) / K2
    grad_hop = jnp.broadcast_to(grad_mean[:, None, :], (seeds_count, K2, hidden_width)).reshape(
        seeds_count * K2, hidden_width
    )
    grad_hidden = jnp.concatenate([grad_seed, grad_hop], 0)
    grad_pre = jnp.where(pre > 0, grad_hidden, 0.0).astype(jnp.bfloat16)
    terms = (
        inner_rows(level_in, grad_pre),
        inner_rows(level_mean, grad_pre),
        inner_rows(hidden_seed, cotangent),
        inner_rows(hidden_mean, cotangent),
    )
    shares = (
        lax.psum_scatter(terms[0], ("clique", "hst"), scatter_dimension=0, tiled=True),
        lax.psum_scatter(terms[1], ("clique", "hst"), scatter_dimension=0, tiled=True),
        lax.psum_scatter(terms[2], ("clique", "hst"), scatter_dimension=0, tiled=True),
        lax.psum_scatter(terms[3], ("clique", "hst"), scatter_dimension=0, tiled=True),
    )
    summed = lax.psum((shares[0], shares[1], shares[2], shares[3]), "dp")
    return (embedding, summed[0], summed[1], summed[2], summed[3])


def solution(mesh):
    in_specs = (
        P("clique", None),
        P("hst", None),
        P(("clique", "dp", "hst"), None),
        P(("clique", "dp", "hst"), None),
        P(("clique", "dp", "hst"), None),
        P(("clique", "dp", "hst"), None, None),
        P(("clique", "dp", "hst"), None),
        P(),
        P(),
        P(),
        P(),
    )
    out_specs = (
        P(("clique", "dp", "hst"), None),
        P(("clique", "hst"), None),
        P(("clique", "hst"), None),
        P(("clique", "hst"), None),
        P(("clique", "hst"), None),
    )
    return jax.shard_map(body, mesh=mesh, in_specs=in_specs, out_specs=out_specs, check_vma=False)
```

profile of v0, /device:TPU:0, one launch (start us, length us, event | category | flops | bytes accessed | tf_op | source)
XLA Modules:
  0.0 513.9 jit_solution(1031296322749675721)
XLA Ops:
  7.3 0.7 all-gather.2.cloned.1.call-update
  8.0 0.6 all_to_all.13
  8.6 5.2 %all-to-all-start = ((s32[4,1,256]{2,1,0:T(1,128)}), s32[4,1,256]{2,1,0:T(1,128)S(1)}, u32[]{:S(2)}, u32[]{:S(2)}) async-start(s32[4,1,256]{2,1,0:T(1,128)} %all_to_all.13), calls=%async_computation | async-start | bytes 8192 | tf_op jit(solution)/shard_map/all_to_all | solution.py:51
  13.8 2.4 convolution_multiply_fusion
  16.2 2.3 all-to-all-done
  18.5 9.4 %gather_fusion = bf16[1024,1024]{1,0:T(8,128)(2,1)} fusion(bf16[2048,1024]{1,0:T(8,128)(2,1)} %param.12, s32[1024]{0:T(1024)S(1)} %broadcast_clamp_fusion), kind=kCustom, calls=%fused_computation | custom fusion | bytes 4198400 | tf_op jit(solution)/shard_map/jit(_take)/gather | solution.py:49
  27.9 3.2 broadcast_select_fusion
  31.1 4.6 all-to-all-start.1
  36.3 1.6 broadcast_in_dim.62
  37.9 3.6 reshape.174
  41.6 0.5 compare_and_fusion.4
  42.1 0.6 compare_and_fusion.2
  42.7 0.6 pad_clamp_fusion
  43.3 0.7 compare_and_fusion
  44.1 3.0 fusion.19
  47.1 12.5 %all-to-all-done.1 = bf16[4,256,1024]{2,1,0:T(8,128)(2,1)} async-done(((bf16[4,256,1024]{2,1,0:T(8,128)(2,1)}), bf16[4,256,1024]{2,1,0:T(8,128)(2,1)}, u32[]{:S(2)}, u32[]{:S(2)}) %all-to-all-start.1) | async-done | bytes 2097184 | tf_op jit(solution)/shard_map/all_to_all | solution.py:54
  59.6 13.0 %pad_maximum_fusion = bf16[5120,1024]{1,0:T(8,128)(2,1)} fusion(bf16[1024,1024]{1,0:T(8,128)(2,1)} %bitcast.4, bf16[4096,1024]{1,0:T(8,128)(2,1)} %all-gather.2.cloned.1.call-done), kind=kLoop, calls=%fused_computation.5 | loop fusion | flops 20971520 | bytes 20971520 | tf_op jit(solution)/shard_map/concatenate | solution.py:55
  72.6 9.2 %gather_fusion.2 = bf16[640,1024]{1,0:T(8,128)(2,1)S(1)} fusion(bf16[5120,1024]{1,0:T(8,128)(2,1)} %pad_maximum_fusion, s32[1024]{0:T(1024)S(1)} %pad_clamp_fusion.1), kind=kCustom, calls=%fused_computation.2 | custom fusion | bytes 2624000 | tf_op jit(solution)/shard_map/jit(_take)/gather | solution.py:57
  81.8 1.6 gather.23
  83.4 1.3 broadcast_select_fusion.1
  84.6 6.8 %gather_fusion.1 = bf16[64,1024]{1,0:T(8,128)(2,1)} fusion(bf16[5120,1024]{1,0:T(8,128)(2,1)} %pad_maximum_fusion, s32[1024]{0:T(1024)S(1)} %pad_clamp_fusion.2), kind=kCustom, calls=%fused_computation.1 | custom fusion | bytes 262400 | tf_op jit(solution)/shard_map/jit(_take)/gather | solution.py:56
  91.4 2.7 convert_reduce_fusion.1
  94.2 0.7 multiply_convert_fusion.2
  94.9 47.5 %gather_fusion.3 = bf16[9600,1024]{1,0:T(8,128)(2,1)} fusion(bf16[5120,1024]{1,0:T(8,128)(2,1)} %pad_maximum_fusion, s32[10240]{0:T(1024)S(1)} %copy-done.9), kind=kCustom, calls=%fused_computation.3 | custom fusion | bytes 39360000 | tf_op jit(solution)/shard_map/jit(_take)/gather | solution.py:58
  142.4 25.7 %gather.25 = bf16[640,15,1024]{2,1,0:T(8,128)(2,1)} reshape(bf16[9600,1024]{1,0:T(8,128)(2,1)} %gather_fusion.3) | data formatting | bytes 39321600 | tf_op jit(solution)/shard_map/jit(_take)/gather | solution.py:58
  168.0 14.7 %convert_reduce_fusion = f32[640,1024]{1,0:T(8,128)S(1)} fusion(bf16[640,15,1024]{2,1,0:T(8,128)(2,1)} %gather.25, pred[640,15]{1,0:T(8,128)(4,1)S(1)} %copy-done.8), kind=kLoop, calls=%fused_computation.4 | loop fusion | flops 28835840 | bytes 22291840 | tf_op jit(solution)/shard_map/reduce_sum | solution.py:12
  183.8 0.6 copy-done.13
  184.9 1.7 fusion.4
  186.6 3.0 fusion
  189.6 1.2 copy-done.20
  190.8 3.8 fusion.2
  194.7 5.3 %fusion.3 = f32[1024,1024]{1,0:T(8,128)} fusion(bf16[704,1024]{1,0:T(8,128)(2,1)} %copy-done.20, bf16[640,1024]{1,0:T(8,128)(2,1)S(1)} %copy-done.4, bf16[64,1024]{1,0:T(8,128)(2,1)} %copy-done.13), kind=kOutput, calls=%fused_computation.22 | convolution fusion | flops 1479278592 | bytes 7077888 | tf_op jit(solution)/shard_map/dot_general | solution.py:21
  200.0 3.2 slice_convert_fusion
  203.2 4.6 reshape.175
  207.8 3.3 reduce_sum.29
  211.1 2.7 fusion.9
  213.9 3.6 fusion.5
  217.5 29.0 %reduce-scatter.7.cloned.1.call-done = f32[128,1024]{1,0:T(8,128)} async-done(((f32[1024,1024]{1,0:T(8,128)}), f32[128,1024]{1,0:T(8,128)}) %reduce-scatter.7.cloned.1.call-update) | async-done | bytes 524304 | tf_op jit(solution)/shard_map/reduce_scatter | solution.py:81
  246.5 55.1 %reduce-scatter.5.cloned.1.call-done = f32[128,1024]{1,0:T(8,128)} async-done(((f32[1024,1024]{1,0:T(8,128)}), f32[128,1024]{1,0:T(8,128)}) %reduce-scatter.5.cloned.1.call-update) | async-done | bytes 524304 | tf_op jit(solution)/shard_map/reduce_scatter | solution.py:80
  301.6 54.6 %reduce-scatter.11.cloned.1.call-done = f32[128,1024]{1,0:T(8,128)} async-done(((f32[1024,1024]{1,0:T(8,128)}), f32[128,1024]{1,0:T(8,128)}) %reduce-scatter.11.cloned.1.call-update) | async-done | bytes 524304 | tf_op jit(solution)/shard_map/reduce_scatter | solution.py:83
  356.2 54.9 %reduce-scatter.9.cloned.1.call-done = f32[128,1024]{1,0:T(8,128)} async-done(((f32[1024,1024]{1,0:T(8,128)}), f32[128,1024]{1,0:T(8,128)}) %reduce-scatter.9.cloned.1.call-update) | async-done | bytes 524304 | tf_op jit(solution)/shard_map/reduce_scatter | solution.py:82
  411.1 2.3 fusion.7
  413.4 1.1 fusion.1
  414.5 87.0 %all-reduce.3.cloned.1.call-done = (f32[128,1024]{1,0:T(8,128)}, f32[128,1024]{1,0:T(8,128)}, f32[128,1024]{1,0:T(8,128)}, f32[128,1024]{1,0:T(8,128)}) async-done(((f32[128,1024]{1,0:T(8,128)}, f32[128,1024]{1,0:T(8,128)}, f32[128,1024]{1,0:T(8,128)}, f32[128,1024]{1,0:T(8,128)}), (f32[128,1024]{1,0:T(8,128)}, f32[128,1024]{1,0:T(8,128)}, f32[128,1024]{1,0:T(8,128)}, ...) | async-done | bytes 2097168 | tf_op jit(solution)/shard_map/psum | solution.py:85
  501.6 2.0 copy.24
  503.6 1.9 copy.25
  505.4 0.8 copy.26
  506.2 0.8 copy.27
  (67 shorter events, 2.6 us)
Async XLA Ops:
  7.2 179.4 %copy-start = (bf16[1024,1024]{1,0:T(8,128)(2,1)S(1)}, bf16[1024,1024]{1,0:T(8,128)(2,1)}, u32[]{:S(2)}) copy-start(bf16[1024,1024]{1,0:T(8,128)(2,1)} %param.19) | copy-start | bytes 6291460
  7.2 0.8 copy-start.16
  7.2 6.6 %copy-start.14 = (s32[1,640]{1,0:T(1,128)S(1)}, s32[1,640]{1,0:T(1,128)}, u32[]{:S(2)}) copy-start(s32[1,640]{1,0:T(1,128)} %param.14) | copy-start | bytes 7684
  7.2 6.6 %copy-start.19 = (s32[1,64]{1,0:T(1,128)S(1)}, s32[1,64]{1,0:T(1,128)}, u32[]{:S(2)}) copy-start(s32[1,64]{1,0:T(1,128)} %param.13) | copy-start | bytes 772
  7.2 6.6 %copy-start.2 = (bf16[64,1024]{1,0:T(8,128)(2,1)S(1)}, bf16[64,1024]{1,0:T(8,128)(2,1)}, u32[]{:S(2)}) copy-start(bf16[64,1024]{1,0:T(8,128)(2,1)} %param.17) | copy-start | bytes 393220
  7.2 52.4 %all-gather.2.cloned.1.call-start = ((), (), s32[]{:S(2)}) async-start(), calls=%async_computation.6 | async-start | bytes 12582912 | tf_op jit(solution)/shard_map/all_gather | solution.py:48
  8.6 9.8 %all-to-all-start = ((s32[4,1,256]{2,1,0:T(1,128)}), s32[4,1,256]{2,1,0:T(1,128)S(1)}, u32[]{:S(2)}, u32[]{:S(2)}) async-start(s32[4,1,256]{2,1,0:T(1,128)} %all_to_all.13), calls=%async_computation | async-start | bytes 8192 | tf_op jit(solution)/shard_map/all_to_all | solution.py:51
  31.1 4.8 copy-start.10
  31.1 28.5 %all-to-all-start.1 = ((bf16[4,256,1024]{2,1,0:T(8,128)(2,1)}), bf16[4,256,1024]{2,1,0:T(8,128)(2,1)}, u32[]{:S(2)}, u32[]{:S(2)}) async-start(bf16[4,256,1024]{2,1,0:T(8,128)(2,1)} %broadcast_select_fusion), calls=%async_computation.1 | async-start | bytes 4194304 | tf_op jit(solution)/shard_map/all_to_all | solution.py:54
  35.7 210.8 %reduce-scatter.7.cloned.1.call-start = ((), (), s32[]{:S(2)}) async-start(), calls=%async_computation.8 | async-start | bytes 4718592 | tf_op jit(solution)/shard_map/reduce_scatter | solution.py:81
  81.8 1.6 copy-start.15
  84.6 10.2 %copy-start.9 = (s32[10240]{0:T(1024)S(1)}, s32[10240]{0:T(1024)}, u32[]{:S(2)}) copy-start(s32[10240]{0:T(1024)} %pad_clamp_fusion) | copy-start | bytes 122884
  142.3 25.7 %copy-start.8 = (pred[640,15]{1,0:T(8,128)(4,1)S(1)}, pred[640,15]{1,0:T(8,128)(4,1)}, u32[]{:S(2)}) copy-start(pred[640,15]{1,0:T(8,128)(4,1)} %compare_and_fusion) | copy-start | bytes 28804
  182.8 0.9 copy-start.5
  182.8 0.9 copy-start.17
  182.8 1.6 copy-start.4
  182.8 2.1 copy-start.18
  183.8 0.7 copy-start.13
  184.9 1.7 copy-start.3
  184.9 1.7 copy-start.11
  184.9 1.7 copy-start.12
  189.6 1.2 copy-start.20
  194.7 106.9 %reduce-scatter.5.cloned.1.call-start = ((), (), s32[]{:S(2)}) async-start(), calls=%async_computation.7 | async-start | bytes 4718592 | tf_op jit(solution)/shard_map/reduce_scatter | solution.py:80
  200.0 156.2 %reduce-scatter.11.cloned.1.call-start = ((), (), s32[]{:S(2)}) async-start(), calls=%async_computation.10 | async-start | bytes 4718592 | tf_op jit(solution)/shard_map/reduce_scatter | solution.py:83
  213.8 197.3 %reduce-scatter.9.cloned.1.call-start = ((), (), s32[]{:S(2)}) async-start(), calls=%async_computation.9 | async-start | bytes 4718592 | tf_op jit(solution)/shard_map/reduce_scatter | solution.py:82
  217.4 284.1 %all-reduce.3.cloned.1.call-start = ((), (), s32[]{:S(2)}) async-start(), calls=%async_computation.11 | async-start | bytes 4194304 | tf_op jit(solution)/shard_map/psum | solution.py:85
  411.1 2.3 copy-start.1
  501.6 3.9 copy-start.7
  501.6 4.7 copy-start.6
Sparse Core Ops, SparseCore 0:
  9.6 22.5 all-gather.1
  194.8 51.6 reduce-scatter.6
  250.2 51.3 reduce-scatter.4
  304.8 51.3 reduce-scatter.10
  359.7 51.2 reduce-scatter.8
  413.5 88.0 all-reduce.2
where the time goes:
time: 516 us; the launch traced here: 514 us
  waiting for transfers between devices  296 us (57%)
  local copies, waits for them, and re-layouts  119 us (23%)
  other arithmetic  45.2 us (9%)
  matrix products  28.8 us (6%)
  between operations  14.4 us (3%)
  starting transfers between devices  9.99 us (2%)
    psum x1, waiting for transfers between devices, body(): summed = lax.psum((shares[0], shares[1], shares[2], shares[3]), 'dp')  87 us
    gather x2, local copies, waits for them, and re-layouts, body(): hop2_feat = jnp.take(lookup, hop2_source[0], axis=0)  73.2 us
    reduce_scatter x1, waiting for transfers between devices, body(): lax.psum_scatter(terms[0], ('clique', 'hst'), scatter_dimension=0, tiled=...  55.1 us
    reduce_scatter x1, waiting for transfers between devices, body(): lax.psum_scatter(terms[2], ('clique', 'hst'), scatter_dimension=0, tiled=...  54.9 us
    reduce_scatter x1, waiting for transfers between devices, body(): lax.psum_scatter(terms[3], ('clique', 'hst'), scatter_dimension=0, tiled=...  54.6 us
    reduce_scatter x1, waiting for transfers between devices, body(): lax.psum_scatter(terms[1], ('clique', 'hst'), scatter_dimension=0, tiled=...  29 us
    reduce_sum x3, other arithmetic, mean_rows(): jnp.sum(values.reshape(groups, fanout, values.shape[1]), axis=1, dtype=jn...  20.8 us
    dot_general x4, matrix products, inner_rows(): lax.dot_general(left, right, (((0,), (0,)), ((), ())), preferred_element_...  15.3 us
  transfers between devices with their start and end apart: 8, of which 7 were waited for; matrix products, arithmetic and copies ran while one was open for 10% of the time, Pallas kernels for 0%

commit v1 on v0

v1 whole, which is shorter than its diff:
```python
import jax
import jax.numpy as jnp
from jax import lax
from jax.experimental import pallas as pl
from jax.experimental.pallas import tpu as pltpu
from jax.sharding import PartitionSpec as P

LANES = 128
F32 = jnp.float32
BF16 = jnp.bfloat16


def inner_rows(left, right):
    return lax.dot_general(left, right, (((0,), (0,)), ((), ())), preferred_element_type=F32)


def inner_cols(left, right):
    return lax.dot_general(left, right, (((1,), (1,)), ((), ())), preferred_element_type=F32)


def matmul(left, right):
    return jnp.dot(left, right, preferred_element_type=F32)


def tree_sum(items):
    while len(items) > 1:
        rest = items[2 * (len(items) // 2):]
        items = [items[i] + items[i + 1] for i in range(0, len(items) - 1, 2)] + rest
    return items[0]


def mean_rows(values, fanout):
    groups = values.shape[0] // fanout
    total = jnp.sum(values.reshape(groups, fanout, values.shape[1]), axis=1, dtype=F32)
    return (total / fanout).astype(BF16)


def pick_kernel(ask_ref, table_ref, out_ref):
    count = ask_ref.shape[0]
    step = 16

    def some(i, carry):
        for j in range(step):
            out_ref[i * step + j] = table_ref[ask_ref[i * step + j]]
        return carry

    lax.fori_loop(0, count // step, some, 0)


def pick_rows(ask, table):
    count, tile = ask.shape[0], table.shape[1:]
    nbytes = (table.shape[0] + count) * tile[0] * tile[1] * 2
    return pl.pallas_call(
        pick_kernel,
        out_shape=jax.ShapeDtypeStruct((count,) + tile, table.dtype),
        in_specs=[
            pl.BlockSpec(memory_space=pltpu.SMEM),
            pl.BlockSpec(memory_space=pltpu.VMEM),
        ],
        out_specs=pl.BlockSpec(memory_space=pltpu.VMEM),
        compiler_params=pltpu.CompilerParams(vmem_limit_bytes=nbytes + (8 << 20)),
        cost_estimate=pl.CostEstimate(flops=0, bytes_accessed=4 * nbytes, transcendentals=0),
        name="pick_rows",
    )(ask, table)


def tree_kernel(seed_ref, hop1_ref, hop2_ref, hot_ref, cold_ref, in_ref, mean_ref, table, sems):
    hot_rows = hot_ref.shape[0]
    seeds, hop1, hop2 = seed_ref.shape[0], hop1_ref.shape[0], hop2_ref.shape[0]
    k2, k1 = hop1 // seeds, hop2 // hop1
    loads = (
        pltpu.make_async_copy(hot_ref, table.at[pl.ds(0, hot_rows)], sems.at[0]),
        pltpu.make_async_copy(cold_ref, table.at[pl.ds(hot_rows, cold_ref.shape[0])], sems.at[1]),
    )
    for load in loads:
        load.start()
    for load in loads:
        load.wait()

    def one_seed(s, carry):
        in_ref[s] = table[seed_ref[s]]
        rows = []
        for j in range(k2):
            row = table[hop1_ref[s * k2 + j]]
            in_ref[seeds + s * k2 + j] = row
            rows.append(row.astype(F32))
        mean_ref[s] = (tree_sum(rows) / k2).astype(BF16)
        return carry

    lax.fori_loop(0, seeds, one_seed, 0)

    def one_node(n, carry):
        for u in range(2):
            m = n * 2 + u
            rows = [table[hop2_ref[m * k1 + j]].astype(F32) for j in range(k1)]
            mean_ref[seeds + m] = (tree_sum(rows) / k1).astype(BF16)
        return carry

    lax.fori_loop(0, hop1 // 2, one_node, 0)


def gather_tree(seed, hop1, hop2, hot, cold):
    tile = hot.shape[1:]
    nodes = seed.shape[0] + hop1.shape[0]
    table_rows = hot.shape[0] + cold.shape[0]
    row_bytes = tile[0] * tile[1] * 2
    out = jax.ShapeDtypeStruct((nodes,) + tile, BF16)
    return pl.pallas_call(
        tree_kernel,
        out_shape=(out, out),
        in_specs=[pl.BlockSpec(memory_space=pltpu.SMEM)] * 3 + [pl.BlockSpec(memory_space=pl.ANY)] * 2,
        out_specs=(pl.BlockSpec(memory_space=pltpu.VMEM),) * 2,
        scratch_shapes=[
            pltpu.VMEM((table_rows,) + tile, BF16),
            pltpu.SemaphoreType.DMA((2,)),
        ],
        compiler_params=pltpu.CompilerParams(
            vmem_limit_bytes=(table_rows + 2 * nodes) * row_bytes + (8 << 20)
        ),
        cost_estimate=pl.CostEstimate(
            flops=0, bytes_accessed=8 * table_rows * row_bytes, transcendentals=0
        ),
        name="gather_tree",
    )(seed, hop1, hop2, hot, cold)


def body(
    hot_table,
    cold_table,
    seed_source,
    hop1_source,
    hop2_source,
    cold_ask,
    cotangent,
    w1_self,
    w1_neigh,
    w2_self,
    w2_neigh,
):
    width = hot_table.shape[1]
    hidden_width = w1_self.shape[1]
    seeds = seed_source.shape[1]
    hop1 = hop1_source.shape[1]
    k2 = hop1 // seeds
    owners, cap = cold_ask.shape[1], cold_ask.shape[2]
    cliques = lax.axis_size("clique")
    hosts = lax.axis_size("hst")
    planes = lax.axis_size("dp")
    tile = (width // LANES, LANES)

    asked = lax.all_to_all(cold_ask[0], "hst", split_axis=0, concat_axis=0, tiled=True)
    hot_tiles = hot_table.reshape((hot_table.shape[0],) + tile)
    hot_full = lax.all_gather(hot_tiles, "clique", axis=0, tiled=True)
    cold_tiles = cold_table.reshape((cold_table.shape[0],) + tile)
    picked = pick_rows(asked.reshape(-1), cold_tiles).reshape((owners, cap) + tile)
    cold_rows = lax.all_to_all(picked, "hst", split_axis=0, concat_axis=0, tiled=True)
    cot_all = lax.all_gather(cotangent, ("clique", "dp", "hst"), axis=0, tiled=True)

    grad_seed = inner_cols(cotangent, w2_self)
    grad_mean = inner_cols(cotangent, w2_neigh) / k2

    in_tiles, mean_tiles = gather_tree(
        seed_source[0], hop1_source[0], hop2_source[0], hot_full, cold_rows.reshape((-1,) + tile)
    )
    level_in = in_tiles.reshape(-1, width)
    level_mean = mean_tiles.reshape(-1, width)

    pre = matmul(level_in, w1_self) + matmul(level_mean, w1_neigh)
    hidden = jnp.maximum(pre, 0.0).astype(BF16)
    hidden_seed = hidden[:seeds]
    hidden_mean = mean_rows(hidden[seeds:], k2)
    embedding = (matmul(hidden_seed, w2_self) + matmul(hidden_mean, w2_neigh)).astype(BF16)

    grad_hop = jnp.broadcast_to(grad_mean[:, None, :], (seeds, k2, hidden_width)).reshape(
        seeds * k2, hidden_width
    )
    grad_hidden = jnp.concatenate([grad_seed, grad_hop], 0)
    grad_pre = jnp.where(pre > 0, grad_hidden, 0.0).astype(BF16)

    me = lax.axis_index("clique")
    half = width // cliques
    share = half // hosts

    def terms(c):
        return [
            inner_rows(lax.dynamic_slice_in_dim(level, c * half, half, 1), grad_pre)
            for level in (level_in, level_mean)
        ]

    total = terms(me)
    for k in range(1, cliques):
        away = [t.astype(BF16) for t in terms(lax.rem(me + k, cliques))]
        pairs = [(c, (c + k) % cliques) for c in range(cliques)]
        got = [lax.ppermute(t, "clique", pairs) for t in away]
        total = [t + g.astype(F32) for t, g in zip(total, got)]
    stacked = jnp.stack([t.astype(BF16).reshape(hosts, share, hidden_width) for t in total], 1)
    parts = lax.all_to_all(stacked, "hst", split_axis=0, concat_axis=0, tiled=True)
    shares = jnp.sum(parts, axis=0, dtype=F32).astype(BF16)
    slabs = lax.all_gather(shares, "dp", axis=0)
    grad_w1 = jnp.sum(slabs, axis=0, dtype=F32)

    shares2 = cliques * hosts
    both = jnp.stack([hidden_seed, hidden_mean], 1).reshape(seeds, 2, shares2, -1)
    both = lax.all_to_all(
        both.transpose(2, 0, 1, 3).reshape(shares2, seeds, -1),
        ("clique", "hst"), split_axis=0, concat_axis=0, tiled=True,
    )
    both = lax.all_gather(both.reshape(cliques, hosts * seeds, -1), "dp", axis=1)
    grad_w2 = inner_rows(both.reshape(cot_all.shape[0], -1), cot_all)
    cut = grad_w2.shape[0] // 2
    return (embedding, grad_w1[0], grad_w1[1], grad_w2[:cut], grad_w2[cut:])


def solution(mesh):
    workers = P(("clique", "dp", "hst"), None)
    rows = P(("clique", "hst"), None)
    in_specs = (
        P("clique", None), P("hst", None), workers, workers, workers,
        P(("clique", "dp", "hst"), None, None), workers, P(), P(), P(), P(),
    )
    return jax.shard_map(
        body, mesh=mesh, in_specs=in_specs, out_specs=(workers, rows, rows, rows, rows), check_vma=False
    )
```

time: 516 us -> 212 us (0.41)
  waiting for transfers between devices: 296 us -> 85.9 us
  local copies, waits for them, and re-layouts: 119 us -> 35.4 us
  other arithmetic: 45.2 us -> 12.4 us
  Pallas kernels: 0 us -> 19.9 us
  starting transfers between devices: 9.99 us -> 18.7 us
    reduce_scatter x4 -> x0, waiting for transfers between devices: 194 us -> none  [the longest x1 55.1 us: body(): lax.psum_scatter(terms[0], ('clique', 'hst'), scatter_dimension=0, tiled=...]
    gather x6 -> x0, local copies, waits for them, and re-layouts: 100 us -> none  [the longest x2 73.2 us: body(): hop2_feat = jnp.take(lookup, hop2_source[0], axis=0)]
    psum x1 -> x0, waiting for transfers between devices: 87 us -> none  [body(): summed = lax.psum((shares[0], shares[1], shares[2], shares[3]), 'dp')]
    all_gather x1 -> x4, waiting for transfers between devices: 0.01 us -> 43.8 us  [the longest x1 42.6 us: body(): slabs = lax.all_gather(shares, 'dp', axis=0)]
    all_to_all x0 -> x2, waiting for transfers between devices: none -> 24.6 us  [the longest x1 24.6 us: body(): lax.all_to_all(stacked, 'hst', split_axis=0, concat_axis=0, tiled=True)]
    pallas_call x0 -> x2, Pallas kernels: none -> 19.9 us  [the longest x1 17.9 us: gather_tree(): pl.pallas_call(tree_kernel, out_shape=(out, out), in_specs=[pl.BlockSpec(...]
    unnamed x46 -> x49, local copies, waits for them, and re-layouts: 8.4 us -> 22.8 us
    concatenate x1 -> x0, other arithmetic: 13 us -> none  [body(): lookup = jnp.concatenate([hot_full, cold_rows.reshape(-1, width)], 0)]
  transfers between devices with their start and end apart: 8 -> 10, of which waited for: 7 -> 4; matrix products, arithmetic and copies ran while one was open for 10% -> 25% of each run, Pallas kernels for 0% -> 9%
where the time goes in v1:
time: 212 us; the launch traced here: 211 us
  waiting for transfers between devices  85.9 us (41%)
  local copies, waits for them, and re-layouts  35.4 us (17%)
  matrix products  24.9 us (12%)
  Pallas kernels  19.9 us (9%)
  starting transfers between devices  18.7 us (9%)
  between operations  14.1 us (7%)
  other arithmetic  12.4 us (6%)
    all_gather x1, waiting for transfers between devices, body(): slabs = lax.all_gather(shares, 'dp', axis=0)  42.6 us
    all_to_all x1, waiting for transfers between devices, body(): lax.all_to_all(stacked, 'hst', split_axis=0, concat_axis=0, tiled=True)  24.6 us
    unnamed x49, local copies, waits for them, and re-layouts  22.8 us
    pallas_call x1, Pallas kernels, gather_tree(): pl.pallas_call(tree_kernel, out_shape=(out, out), in_specs=[pl.BlockSpec(...  17.9 us
    all_to_all x1, waiting for transfers between devices, body(): lax.all_to_all(picked, 'hst', split_axis=0, concat_axis=0, tiled=True)  16 us
    dot_general x5, matrix products, inner_rows(): lax.dot_general(left, right, (((0,), (0,)), ((), ())), preferred_element_...  13.3 us
    dot_general x4, matrix products, matmul(): return jnp.dot(left, right, preferred_element_type=F32)  6.21 us
    dot_general x2, matrix products, inner_cols(): lax.dot_general(left, right, (((1,), (1,)), ((), ())), preferred_element_...  5.44 us
  transfers between devices with their start and end apart: 10, of which 4 were waited for; matrix products, arithmetic and copies ran while one was open for 25% of the time, Pallas kernels for 9%

profile of v1, /device:TPU:0, one launch (start us, length us, event | category | flops | bytes accessed | tf_op | source)
XLA Modules:
  0.0 211.4 jit_solution(13424344140497680275)
XLA Ops:
  7.2 5.4 %copy.24 = bf16[256,8,8,128]{3,2,1,0:T(8,128)(2,1)} copy(bf16[256,8,8,128]{3,1,2,0:T(8,128)(2,1)} %bitcast.71) | data formatting | bytes 8388608
  12.7 0.7 all-gather.10.cloned.1.call-update
  13.4 0.6 all_to_all.15
  14.0 5.2 %all-to-all-start = ((s32[4,1,256]{2,1,0:T(1,128)}), s32[4,1,256]{2,1,0:T(1,128)S(1)}, u32[]{:S(2)}, u32[]{:S(2)}) async-start(s32[4,1,256]{2,1,0:T(1,128)} %all_to_all.15), calls=%async_computation | async-start | bytes 8192 | tf_op jit(solution)/shard_map/all_to_all | solution.py:151
  19.1 5.5 %copy.25 = bf16[256,8,8,128]{3,2,1,0:T(8,128)(2,1)} copy(bf16[256,8,8,128]{3,1,2,0:T(8,128)(2,1)} %bitcast.72) | data formatting | bytes 8388608
  24.7 2.9 %copy-done.2 = bf16[256,8,8,128]{3,2,1,0:T(8,128)(2,1)S(1)} copy-done((bf16[256,8,8,128]{3,2,1,0:T(8,128)(2,1)S(1)}, bf16[256,8,8,128]{3,2,1,0:T(8,128)(2,1)}, u32[]{:S(2)}) %copy-start.2) | copy-done | bytes 4194328
  27.6 2.0 pick_rows.1
  29.6 1.3 copy-done.4
  30.9 4.8 %all-to-all-start.1 = ((bf16[4,256,8,128]{3,2,1,0:T(8,128)(2,1)}), bf16[4,256,8,128]{3,2,1,0:T(8,128)(2,1)}, u32[]{:S(2)}, u32[]{:S(2)}) async-start(bf16[4,256,8,128]{3,2,1,0:T(8,128)(2,1)} %bitcast.63), calls=%async_computation.1 | async-start | bytes 4194304 | tf_op jit(solution)/shard_map/all_to_all | solution.py:156
  35.8 2.4 %convolution_multiply_fusion = bf16[64,1024]{1,0:T(8,128)(2,1)S(1)} fusion(bf16[64,1024]{1,0:T(8,128)(2,1)S(1)} %copy-done.12, bf16[1024,1024]{1,0:T(8,128)(2,1)} %param.21), kind=kOutput, calls=%fused_computation.13 | convolution fusion | flops 134348800 | bytes 2359296 | tf_op jit(solution)/shard_map/dot_general | solution.py:18
  38.2 1.6 broadcast_in_dim.3
  39.8 2.6 %reshape.76 = bf16[640,1024]{1,0:T(8,128)(2,1)S(1)} reshape(bf16[64,10,1024]{2,1,0:T(8,128)(2,1)} %broadcast_in_dim.3) | data formatting | bytes 2621440 | tf_op jit(solution)/shard_map/reshape | solution.py:174
  42.4 3.1 %fusion.22 = bf16[64,1024]{1,0:T(8,128)(2,1)} fusion(bf16[64,1024]{1,0:T(8,128)(2,1)} %param.17, bf16[1024,1024]{1,0:T(8,128)(2,1)} %param.20), kind=kOutput, calls=%fused_computation.37 | convolution fusion | flops 134217728 | bytes 2359296 | tf_op jit(solution)/shard_map/dot_general | solution.py:18
  45.5 16.0 %all-to-all-done.1 = bf16[4,256,8,128]{3,2,1,0:T(8,128)(2,1)} async-done(((bf16[4,256,8,128]{3,2,1,0:T(8,128)(2,1)}), bf16[4,256,8,128]{3,2,1,0:T(8,128)(2,1)}, u32[]{:S(2)}, u32[]{:S(2)}) %all-to-all-start.1) | async-done | bytes 2097184 | tf_op jit(solution)/shard_map/all_to_all | solution.py:156
  61.5 3.4 %copy-done.3 = bf16[4096,8,128]{2,1,0:T(8,128)(2,1)S(1)} copy-done((bf16[4096,8,128]{2,1,0:T(8,128)(2,1)S(1)}, bf16[4096,8,128]{2,1,0:T(8,128)(2,1)}, u32[]{:S(2)}) %copy-start.3) | copy-done | bytes 8388632
  64.9 17.9 %gather_tree.1 = (bf16[704,8,128]{2,1,0:T(8,128)(2,1)S(1)}, bf16[704,8,128]{2,1,0:T(8,128)(2,1)S(1)}) custom-call(s32[64]{0:T(128)S(1)} %bitcast.69, s32[640]{0:T(1024)S(1)} %reduce.1.hop1_ref, s32[9600]{0:T(1024)S(1)} %reduce.2.hop2_ref, bf16[4096,8,128]{2,1,0:T(8,128)(2,1)S(1)} %copy-done.3, bf16[1024,8,128]{2,1,0:T(8,128)(2,1)} %bitcast.3.cold_ref), custom_call_target="tpu_custom_call" | custom-call | bytes 83886080 | tf_op jit(solution)/shard_map/gather_tree/pallas_call | solution.py:108
  82.8 0.4 copy.37
  83.3 0.4 copy.36
  83.7 1.7 copy-done.18
  85.4 1.7 fusion.20
  87.1 1.9 fusion
  89.0 2.0 convolution_convert_fusion.1
  91.0 2.0 convolution_convert_fusion
  93.1 0.5 collective-permute-start.1
  93.5 1.9 slice_convert_fusion
  95.4 4.4 %reshape.79 = f32[64,10,1024]{2,1,0:T(8,128)} reshape(f32[640,1024]{1,0:T(8,128)} %slice_convert_fusion) | data formatting | bytes 5242880 | tf_op jit(solution)/shard_map/convert_element_type | solution.py:34
  99.8 3.1 %reduce_sum.30 = f32[64,1024]{1,0:T(8,128)S(1)} reduce(f32[64,10,1024]{2,1,0:T(8,128)} %reshape.79, f32[]{:T(128)} %constant.9.clone.1), dimensions={1}, to_apply=%region_0.0 | reduce | flops 589824 | bytes 2883588 | tf_op jit(solution)/shard_map/reduce_sum | solution.py:34
  103.2 0.9 slice_bitcast_fusion.2
  104.3 0.6 maximum_bitcast_fusion
  104.9 0.9 reshape.77
  105.8 3.4 %all-to-all-start.3 = ((bf16[8,64,256]{2,1,0:T(8,128)(2,1)}), bf16[8,64,256]{2,1,0:T(8,128)(2,1)S(1)}, u32[]{:S(2)}, u32[]{:S(2)}) async-start(bf16[8,64,256]{2,1,0:T(8,128)(2,1)} %reshape.77), calls=%async_computation.3 | async-start | bytes 524288 | tf_op jit(solution)/shard_map/all_to_all | solution.py:204
  109.3 3.1 %add_convert_fusion.1 = bf16[512,1024]{1,0:T(8,128)(2,1)S(1)} fusion(bf16[512,1024]{1,0:T(8,128)(2,1)} %collective-permute-done, bf16[704,1024]{1,0:T(8,128)(2,1)} %copy-done.19, bf16[704,1024]{1,0:T(8,128)(2,1)} %bitcast.77, s32[]{:T(128)S(6)} %select_n.12), kind=kOutput, calls=%fused_computation.6 | convolution fusion | flops 739770368 | bytes 4259844 | tf_op jit(solution)/shard_map/dot_general | solution.py:14
  112.4 2.3 %add_convert_fusion = bf16[512,1024]{1,0:T(8,128)(2,1)S(1)} fusion(bf16[512,1024]{1,0:T(8,128)(2,1)} %collective-permute-done.1, bf16[704,1024]{1,0:T(8,128)(2,1)S(1)} %copy-done.20, bf16[704,1024]{1,0:T(8,128)(2,1)S(1)} %bitcast.75, s32[]{:T(128)S(6)} %select_n.12), kind=kOutput, calls=%fused_computation.5 | convolution fusion | flops 739770368 | bytes 4259844 | tf_op jit(solution)/shard_map/dot_general | solution.py:14
  114.7 1.5 pad_maximum_fusion
  116.2 0.7 copy-done.13
  116.9 4.5 %all-to-all-start.2 = ((bf16[4,2,128,1024]{3,2,1,0:T(8,128)(2,1)}), bf16[4,2,128,1024]{3,2,1,0:T(8,128)(2,1)}, u32[]{:S(2)}, u32[]{:S(2)}) async-start(bf16[4,2,128,1024]{3,2,1,0:T(8,128)(2,1)} %pad_maximum_fusion), calls=%async_computation.2 | async-start | bytes 4194304 | tf_op jit(solution)/shard_map/all_to_all | solution.py:197
  121.5 0.7 all-gather.8.cloned.1.call-update
  122.2 0.3 all-gather.12.cloned.1.call-start
  122.4 24.6 %all-to-all-done.2 = bf16[4,2,128,1024]{3,2,1,0:T(8,128)(2,1)} async-done(((bf16[4,2,128,1024]{3,2,1,0:T(8,128)(2,1)}), bf16[4,2,128,1024]{3,2,1,0:T(8,128)(2,1)}, u32[]{:S(2)}, u32[]{:S(2)}) %all-to-all-start.2) | async-done | bytes 2097184 | tf_op jit(solution)/shard_map/all_to_all | solution.py:197
  147.1 2.9 %reduce_sum.31 = bf16[2,128,1024]{2,1,0:T(8,128)(2,1)} reduce(bf16[4,2,128,1024]{3,2,1,0:T(8,128)(2,1)} %all-to-all-done.2, bf16[]{:T(256)} %constant.25.clone.1), dimensions={0}, to_apply=%region_1.2 | reduce | flops 786432 | bytes 2621442 | tf_op jit(solution)/shard_map/reduce_sum | solution.py:198
  150.0 1.5 fusion.12
  151.7 1.1 fusion.1
  152.8 1.3 all-gather.8.cloned.1.call-done
  154.1 3.8 %fusion.23 = f32[256,1024]{1,0:T(8,128)S(1)} fusion(bf16[2048,256]{1,0:T(8,128)(2,1)} %bitcast.83, bf16[2048,1024]{1,0:T(8,128)(2,1)} %all-gather.10.cloned.1.call-done), kind=kOutput, calls=%fused_computation.38 | convolution fusion | flops 1073741824 | bytes 6291456 | tf_op jit(solution)/shard_map/dot_general | solution.py:14
  157.9 1.1 fusion.21
  159.0 42.6 %all-gather.12.cloned.1.call-done = bf16[8,128,1024]{2,1,0:T(8,128)(2,1)} async-done(((bf16[2,128,1024]{2,1,0:T(8,128)(2,1)}), bf16[8,128,1024]{2,1,0:T(8,128)(2,1)}) %all-gather.12.cloned.1.call-update) | async-done | bytes 2097168 | tf_op jit(solution)/shard_map/all_gather | solution.py:199
  201.5 2.3 %convert_reduce_fusion = f32[2,128,1024]{2,1,0:T(8,128)S(1)} fusion(bf16[4,2,128,1024]{3,2,1,0:T(8,128)(2,1)} %bitcast.73), kind=kLoop, calls=%fused_computation | loop fusion | flops 1835008 | bytes 3145728 | tf_op jit(solution)/shard_map/reduce_sum | solution.py:200
  203.8 1.0 slice_bitcast_fusion
  (56 shorter events, 1.0 us)
Async XLA Ops:
  7.2 79.9 %copy-start = (bf16[1024,1024]{1,0:T(8,128)(2,1)S(1)}, bf16[1024,1024]{1,0:T(8,128)(2,1)}, u32[]{:S(2)}) copy-start(bf16[1024,1024]{1,0:T(8,128)(2,1)} %param.19) | copy-start | bytes 6291460
  7.2 54.3 %all-gather.6.cloned.1.call-start = ((), (), s32[]{:S(2)}) async-start(), calls=%async_computation.4 | async-start | bytes 12582912 | tf_op jit(solution)/shard_map/all_gather | solution.py:153
  12.6 0.8 copy-start.16
  12.6 140.2 %all-gather.10.cloned.1.call-start = ((), (), s32[]{:S(2)}) async-start(), calls=%async_computation.6 | async-start | bytes 4325376 | tf_op jit(solution)/shard_map/all_gather | solution.py:157
  14.0 10.7 %all-to-all-start = ((s32[4,1,256]{2,1,0:T(1,128)}), s32[4,1,256]{2,1,0:T(1,128)S(1)}, u32[]{:S(2)}, u32[]{:S(2)}) async-start(s32[4,1,256]{2,1,0:T(1,128)} %all_to_all.15), calls=%async_computation | async-start | bytes 8192 | tf_op jit(solution)/shard_map/all_to_all | solution.py:151
  24.7 2.9 %copy-start.2 = (bf16[256,8,8,128]{3,2,1,0:T(8,128)(2,1)S(1)}, bf16[256,8,8,128]{3,2,1,0:T(8,128)(2,1)}, u32[]{:S(2)}) copy-start(bf16[256,8,8,128]{3,2,1,0:T(8,128)(2,1)} %copy.25) | copy-start | bytes 12582916
  29.6 1.3 copy-start.4
  30.9 4.8 %copy-start.15 = (s32[1,9600]{1,0:T(1,128)S(1)}, s32[1,9600]{1,0:T(1,128)}, u32[]{:S(2)}) copy-start(s32[1,9600]{1,0:T(1,128)} %param.15) | copy-start | bytes 115204
  30.9 4.9 %copy-start.17 = (s32[1,640]{1,0:T(1,128)S(1)}, s32[1,640]{1,0:T(1,128)}, u32[]{:S(2)}) copy-start(s32[1,640]{1,0:T(1,128)} %param.14) | copy-start | bytes 7684
  30.9 4.9 %copy-start.12 = (bf16[64,1024]{1,0:T(8,128)(2,1)S(1)}, bf16[64,1024]{1,0:T(8,128)(2,1)}, u32[]{:S(2)}) copy-start(bf16[64,1024]{1,0:T(8,128)(2,1)} %param.17) | copy-start | bytes 393220
  30.9 30.6 %all-to-all-start.1 = ((bf16[4,256,8,128]{3,2,1,0:T(8,128)(2,1)}), bf16[4,256,8,128]{3,2,1,0:T(8,128)(2,1)}, u32[]{:S(2)}, u32[]{:S(2)}) async-start(bf16[4,256,8,128]{3,2,1,0:T(8,128)(2,1)} %bitcast.63), calls=%async_computation.1 | async-start | bytes 4194304 | tf_op jit(solution)/shard_map/all_to_all | solution.py:156
  39.8 21.7 %copy-start.5 = (s32[1,64]{1,0:T(1,128)S(1)}, s32[1,64]{1,0:T(1,128)}, u32[]{:S(2)}) copy-start(s32[1,64]{1,0:T(1,128)} %param.13) | copy-start | bytes 772
  61.5 3.4 %copy-start.3 = (bf16[4096,8,128]{2,1,0:T(8,128)(2,1)S(1)}, bf16[4096,8,128]{2,1,0:T(8,128)(2,1)}, u32[]{:S(2)}) copy-start(bf16[4096,8,128]{2,1,0:T(8,128)(2,1)} %all-gather.6.cloned.1.call-done.hot_ref) | copy-start | bytes 25165828
  83.3 5.7 %copy-start.11 = (bf16[88,8,8,128]{3,1,2,0:T(8,128)(2,1)}, bf16[88,8,8,128]{3,1,2,0:T(8,128)(2,1)S(1)}, u32[]{:S(2)}) copy-start(bf16[88,8,8,128]{3,1,2,0:T(8,128)(2,1)S(1)} %copy.37) | copy-start | bytes 4325380
  83.3 2.1 %copy-start.18 = (bf16[1024,1024]{1,0:T(8,128)(2,1)S(1)}, bf16[1024,1024]{1,0:T(8,128)(2,1)}, u32[]{:S(2)}) copy-start(bf16[1024,1024]{1,0:T(8,128)(2,1)} %param.18) | copy-start | bytes 6291460
  85.4 5.7 %copy-start.9 = (bf16[88,8,8,128]{3,1,2,0:T(8,128)(2,1)}, bf16[88,8,8,128]{3,1,2,0:T(8,128)(2,1)S(1)}, u32[]{:S(2)}) copy-start(bf16[88,8,8,128]{3,1,2,0:T(8,128)(2,1)S(1)} %copy.36) | copy-start | bytes 4325380
  85.4 1.7 copy-start.14
  89.0 2.1 copy-start.19
  89.0 4.6 %copy-start.8 = (bf16[704,1024]{1,0:T(8,128)(2,1)}, bf16[704,1024]{1,0:T(8,128)(2,1)S(1)}, u32[]{:S(2)}) copy-start(bf16[704,1024]{1,0:T(8,128)(2,1)S(1)} %get-tuple-element.10) | copy-start | bytes 4325380
  91.0 18.2 %collective-permute-start = (bf16[512,1024]{1,0:T(8,128)(2,1)}, bf16[512,1024]{1,0:T(8,128)(2,1)}, u32[]{:S(2)}, u32[]{:S(2)}) collective-permute-start(bf16[512,1024]{1,0:T(8,128)(2,1)} %convolution_convert_fusion.1), channel_id=1, source_target_pairs={{0,16},{16,0},{1,17},{17,1},{2,18},{18,2},{3,19},{19,3},{4,20},{20... | collective-permute-start | bytes 3145736 | tf_op jit(solution)/shard_map/ppermute | solution.py:194
  93.1 19.4 %collective-permute-start.1 = (bf16[512,1024]{1,0:T(8,128)(2,1)}, bf16[512,1024]{1,0:T(8,128)(2,1)}, u32[]{:S(2)}, u32[]{:S(2)}) collective-permute-start(bf16[512,1024]{1,0:T(8,128)(2,1)} %convolution_convert_fusion), channel_id=1, source_target_pairs={{0,16},{16,0},{1,17},{17,1},{2,18},{18,2},{3,19},{19,3},{4,20},{20... | collective-permute-start | bytes 3145736 | tf_op jit(solution)/shard_map/ppermute | solution.py:194
  105.8 10.4 %all-to-all-start.3 = ((bf16[8,64,256]{2,1,0:T(8,128)(2,1)}), bf16[8,64,256]{2,1,0:T(8,128)(2,1)S(1)}, u32[]{:S(2)}, u32[]{:S(2)}) async-start(bf16[8,64,256]{2,1,0:T(8,128)(2,1)} %reshape.77), calls=%async_computation.3 | async-start | bytes 524288 | tf_op jit(solution)/shard_map/all_to_all | solution.py:204
  109.2 3.2 %copy-start.10 = (bf16[88,8,8,128]{3,1,2,0:T(8,128)(2,1)S(1)}, bf16[88,8,8,128]{3,1,2,0:T(8,128)(2,1)}, u32[]{:S(2)}) copy-start(bf16[88,8,8,128]{3,1,2,0:T(8,128)(2,1)} %copy-done.9) | copy-start | bytes 4325380
  109.3 3.2 %copy-start.20 = (bf16[704,1024]{1,0:T(8,128)(2,1)S(1)}, bf16[704,1024]{1,0:T(8,128)(2,1)}, u32[]{:S(2)}) copy-start(bf16[704,1024]{1,0:T(8,128)(2,1)} %copy-done.19) | copy-start | bytes 4325380
  116.2 0.7 copy-start.13
  116.9 30.1 %all-to-all-start.2 = ((bf16[4,2,128,1024]{3,2,1,0:T(8,128)(2,1)}), bf16[4,2,128,1024]{3,2,1,0:T(8,128)(2,1)}, u32[]{:S(2)}, u32[]{:S(2)}) async-start(bf16[4,2,128,1024]{3,2,1,0:T(8,128)(2,1)} %pad_maximum_fusion), calls=%async_computation.2 | async-start | bytes 4194304 | tf_op jit(solution)/shard_map/all_to_all | solution.py:197
  121.4 28.6 %copy-start.6 = (bf16[1024,1024]{1,0:T(8,128)(2,1)S(1)}, bf16[1024,1024]{1,0:T(8,128)(2,1)}, u32[]{:S(2)}) copy-start(bf16[1024,1024]{1,0:T(8,128)(2,1)} %param.20) | copy-start | bytes 6291460
  121.4 32.7 %all-gather.8.cloned.1.call-start = ((), (), s32[]{:S(2)}) async-start(), calls=%async_computation.5 | async-start | bytes 1310720 | tf_op jit(solution)/shard_map/all_gather | solution.py:208
  122.2 79.4 %all-gather.12.cloned.1.call-start = ((), (), s32[]{:S(2)}) async-start(), calls=%async_computation.7 | async-start | bytes 2621440 | tf_op jit(solution)/shard_map/all_gather | solution.py:199
  150.0 1.7 copy-start.7
  201.5 3.3 %copy-start.1 = (bf16[1024,1024]{1,0:T(8,128)(2,1)S(1)}, bf16[1024,1024]{1,0:T(8,128)(2,1)}, u32[]{:S(2)}) copy-start(bf16[1024,1024]{1,0:T(8,128)(2,1)} %param.19) | copy-start | bytes 6291460
Sparse Core Ops, SparseCore 0:
  12.7 22.5 all-gather.5
  38.3 72.8 all-gather.9
  124.4 29.6 all-gather.7
  156.1 45.3 all-gather.11

commit v2 on v1

--- a/solution.py
+++ b/solution.py
@@ -27,12 +27,6 @@
         rest = items[2 * (len(items) // 2):]
         items = [items[i] + items[i + 1] for i in range(0, len(items) - 1, 2)] + rest
     return items[0]
-
-
-def mean_rows(values, fanout):
-    groups = values.shape[0] // fanout
-    total = jnp.sum(values.reshape(groups, fanout, values.shape[1]), axis=1, dtype=F32)
-    return (total / fanout).astype(BF16)
 
 
 def pick_kernel(ask_ref, table_ref, out_ref):
@@ -124,6 +118,112 @@
     )(seed, hop1, hop2, hot, cold)
 
 
+def reduce_kernel(
+    mine0, mine1, away0, away1, out0, out1,
+    got1, send2, got2, keep, send3, got3, send4, got4,
+    s1, r1, s2, r2, s3, r3, s4, r4,
+):
+    mine, away, out = (mine0, mine1), (away0, away1), (out0, out1)
+    hosts, planes = mine0.shape[0], mine0.shape[1]
+    c, d, h = lax.axis_index("clique"), lax.axis_index("dp"), lax.axis_index("hst")
+    host = [lax.rem(h + k, hosts) for k in range(hosts)]
+    plane = [lax.rem(d + k, planes) for k in range(planes)]
+    peers = [{"clique": 1 - c}] + [{"hst": q} for q in host[1:]] + [{"dp": p} for p in plane[1:]]
+
+    barrier = pltpu.get_barrier_semaphore()
+    for peer in peers:
+        pl.semaphore_signal(barrier, inc=1, device_id=peer, device_id_type=pl.DeviceIdType.MESH)
+    pl.semaphore_wait(barrier, len(peers))
+
+    def send(src, dst, sent, landed, peer):
+        copy = pltpu.make_async_remote_copy(
+            src_ref=src, dst_ref=dst, send_sem=sent, recv_sem=landed,
+            device_id=peer, device_id_type=pl.DeviceIdType.MESH,
+        )
+        copy.start()
+        return copy
+
+    first, second, third, fourth = {}, {}, {}, {}
+    for m in range(2):
+        for k in list(range(1, hosts)) + [0]:
+            q = host[k]
+            first[m, k] = send(
+                away[m].at[q], got1.at[m, q], s1.at[m, k], r1.at[m, k], {"clique": 1 - c}
+            )
+    for m in range(2):
+        for k in range(1, hosts):
+            q = host[k]
+            first[m, k].wait_recv()
+            for p in range(planes):
+                send2[m, k - 1, p] = (mine[m][q, p] + got1[m, q, p].astype(F32)).astype(BF16)
+            second[m, k] = send(
+                send2.at[m, k - 1], got2.at[m, k - 1], s2.at[m, k - 1], r2.at[m, k - 1], {"hst": q}
+            )
+        first[m, 0].wait_recv()
+    for m in range(2):
+        for k in range(1, hosts):
+            second[m, k].wait_recv()
+        for p in range(planes):
+            total = mine[m][h, p] + got1[m, h, p].astype(F32)
+            for k in range(1, hosts):
+                total = total + got2[m, k - 1, p].astype(F32)
+            keep[m, p] = total
+            send3[m, p] = total.astype(BF16)
+        for k in range(1, planes):
+            third[m, k] = send(
+                send3.at[m, plane[k]], got3.at[m, k - 1], s3.at[m, k - 1], r3.at[m, k - 1],
+                {"dp": plane[k]},
+            )
+    for m in range(2):
+        for k in range(1, planes):
+            third[m, k].wait_recv()
+        total = keep[m, d]
+        for k in range(1, planes):
+            total = total + got3[m, k - 1].astype(F32)
+        send4[m] = total.astype(BF16)
+        for k in range(1, planes):
+            fourth[m, k] = send(
+                send4.at[m], got4.at[m, k - 1], s4.at[m, k - 1], r4.at[m, k - 1], {"dp": plane[k]}
+            )
+        out[m][d] = send4[m].astype(F32)
+    for m in range(2):
+        for k in range(1, planes):
+            fourth[m, k].wait_recv()
+            out[m][lax.rem(d + planes - k, planes)] = got4[m, k - 1].astype(F32)
+    for copies in (first, second, third, fourth):
+        for copy in copies.values():
+            copy.wait_send()
+
+
+def reduce_pair(mine, away):
+    hosts, planes, rows, width = mine[0].shape
+    out = jax.ShapeDtypeStruct((planes, rows, width), F32)
+    piece = (rows, width)
+    return pl.pallas_call(
+        reduce_kernel,
+        out_shape=(out, out),
+        in_specs=[pl.BlockSpec(memory_space=pltpu.VMEM)] * 4,
+        out_specs=(pl.BlockSpec(memory_space=pltpu.VMEM),) * 2,
+        scratch_shapes=[
+            pltpu.VMEM((2, hosts, planes) + piece, BF16),
+            pltpu.VMEM((2, hosts - 1, planes) + piece, BF16),
+            pltpu.VMEM((2, hosts - 1, planes) + piece, BF16),
+            pltpu.VMEM((2, planes) + piece, F32),
+            pltpu.VMEM((2, planes) + piece, BF16),
+            pltpu.VMEM((2, planes - 1) + piece, BF16),
+            pltpu.VMEM((2,) + piece, BF16),
+            pltpu.VMEM((2, planes - 1) + piece, BF16),
+            pltpu.SemaphoreType.DMA((2, hosts)),
+            pltpu.SemaphoreType.DMA((2, hosts)),
+        ] + [pltpu.SemaphoreType.DMA((2, hosts - 1))] * 2 + [pltpu.SemaphoreType.DMA((2, planes - 1))] * 4,
+        compiler_params=pltpu.CompilerParams(
+            collective_id=0, has_side_effects=True, vmem_limit_bytes=40 << 20
+        ),
+        cost_estimate=pl.CostEstimate(flops=0, bytes_accessed=100 << 20, transcendentals=0),
+        name="reduce_pair",
+    )(*mine, *away)
+
+
 def body(
     hot_table,
     cold_table,
@@ -168,7 +268,9 @@
     pre = matmul(level_in, w1_self) + matmul(level_mean, w1_neigh)
     hidden = jnp.maximum(pre, 0.0).astype(BF16)
     hidden_seed = hidden[:seeds]
-    hidden_mean = mean_rows(hidden[seeds:], k2)
+    node = lax.broadcasted_iota(jnp.int32, (seeds, hop1), 1) // k2
+    member = (node == lax.broadcasted_iota(jnp.int32, (seeds, hop1), 0)).astype(BF16)
+    hidden_mean = (matmul(member, hidden[seeds:]) / k2).astype(BF16)
     embedding = (matmul(hidden_seed, w2_self) + matmul(hidden_mean, w2_neigh)).astype(BF16)
 
     grad_hop = jnp.broadcast_to(grad_mean[:, None, :], (seeds, k2, hidden_width)).reshape(
@@ -176,28 +278,6 @@
     )
     grad_hidden = jnp.concatenate([grad_seed, grad_hop], 0)
     grad_pre = jnp.where(pre > 0, grad_hidden, 0.0).astype(BF16)
-
-    me = lax.axis_index("clique")
-    half = width // cliques
-    share = half // hosts
-
-    def terms(c):
-        return [
-            inner_rows(lax.dynamic_slice_in_dim(level, c * half, half, 1), grad_pre)
-            for level in (level_in, level_mean)
-        ]
-
-    total = terms(me)
-    for k in range(1, cliques):
-        away = [t.astype(BF16) for t in terms(lax.rem(me + k, cliques))]
-        pairs = [(c, (c + k) % cliques) for c in range(cliques)]
-        got = [lax.ppermute(t, "clique", pairs) for t in away]
-        total = [t + g.astype(F32) for t, g in zip(total, got)]
-    stacked = jnp.stack([t.astype(BF16).reshape(hosts, share, hidden_width) for t in total], 1)
-    parts = lax.all_to_all(stacked, "hst", split_axis=0, concat_axis=0, tiled=True)
-    shares = jnp.sum(parts, axis=0, dtype=F32).astype(BF16)
-    slabs = lax.all_gather(shares, "dp", axis=0)
-    grad_w1 = jnp.sum(slabs, axis=0, dtype=F32)
 
     shares2 = cliques * hosts
     both = jnp.stack([hidden_seed, hidden_mean], 1).reshape(seeds, 2, shares2, -1)
@@ -207,6 +287,22 @@
     )
     both = lax.all_gather(both.reshape(cliques, hosts * seeds, -1), "dp", axis=1)
     grad_w2 = inner_rows(both.reshape(cot_all.shape[0], -1), cot_all)
+
+    me = lax.axis_index("clique")
+    half = width // cliques
+    rows = half // hosts // planes
+
+    def terms(c):
+        return [
+            inner_rows(lax.dynamic_slice_in_dim(level, c * half, half, 1), grad_pre).reshape(
+                hosts, planes, rows, hidden_width
+            )
+            for level in (level_in, level_mean)
+        ]
+
+    away = [t.astype(BF16) for t in terms(1 - me)]
+    grad_w1 = [t.reshape(-1, hidden_width) for t in reduce_pair(terms(me), away)]
+
     cut = grad_w2.shape[0] // 2
     return (embedding, grad_w1[0], grad_w1[1], grad_w2[:cut], grad_w2[cut:])
 

time: 212 us -> 181 us (0.85)
  waiting for transfers between devices: 85.9 us -> 21.8 us
  Pallas kernels: 19.9 us -> 70 us
  other arithmetic: 12.4 us -> 2.6 us
  starting transfers between devices: 18.7 us -> 13.4 us
  matrix products: 24.9 us -> 22.6 us
    pallas_call x0 -> x1, Pallas kernels: none -> 50.1 us  [reduce_pair(): pl.pallas_call(reduce_kernel, out_shape=(out, out), in_specs=[pl.BlockSpe...]
    all_gather x1 -> x0, waiting for transfers between devices: 42.6 us -> none  [body(): slabs = lax.all_gather(shares, 'dp', axis=0)]
    all_to_all x1 -> x0, waiting for transfers between devices: 24.6 us -> none  [body(): lax.all_to_all(stacked, 'hst', split_axis=0, concat_axis=0, tiled=True)]
    reduce_sum x3 -> x0, other arithmetic: 8.3 us -> none  [the longest x1 3.13 us: mean_rows(): jnp.sum(values.reshape(groups, fanout, values.shape[1]), axis=1, dtype=F32)]
    all_to_all x1, waiting for transfers between devices: 0.01 us -> 7.23 us  [body(): lax.all_to_all(both.transpose(2, 0, 1, 3).reshape(shares2, seeds, -1), ('...]
    convert_element_type x2 -> x0, local copies, waits for them, and re-layouts: 4.57 us -> none  [the longest x1 4.37 us: mean_rows(): jnp.sum(values.reshape(groups, fanout, values.shape[1]), axis=1, dtype=F32)]
    all_to_all x1 -> x0, starting transfers between devices: 4.46 us -> none  [body(): lax.all_to_all(stacked, 'hst', split_axis=0, concat_axis=0, tiled=True)]
    dot_general x5, matrix products: 13.3 us -> 9.59 us  [inner_rows(): lax.dot_general(left, right, (((0,), (0,)), ((), ())), preferred_element_...]
  transfers between devices with their start and end apart: 10 -> 6, of which waited for: 4 -> 2; matrix products, arithmetic and copies ran while one was open for 25% -> 20% of each run, Pallas kernels for 9% -> 39%
where the time goes in v2:
time: 181 us; the launch traced here: 180 us
  Pallas kernels  70 us (39%)
  local copies, waits for them, and re-layouts  35.2 us (19%)
  matrix products  22.6 us (12%)
  waiting for transfers between devices  21.8 us (12%)
  between operations  14.1 us (8%)
  starting transfers between devices  13.4 us (7%)
  other arithmetic  2.6 us (1%)
    pallas_call x1, Pallas kernels, reduce_pair(): pl.pallas_call(reduce_kernel, out_shape=(out, out), in_specs=[pl.BlockSpe...  50.1 us
    unnamed x59, local copies, waits for them, and re-layouts  26 us
    pallas_call x1, Pallas kernels, gather_tree(): pl.pallas_call(tree_kernel, out_shape=(out, out), in_specs=[pl.BlockSpec(...  17.9 us
    all_to_all x1, waiting for transfers between devices, body(): lax.all_to_all(picked, 'hst', split_axis=0, concat_axis=0, tiled=True)  13.8 us
    dot_general x5, matrix products, inner_rows(): lax.dot_general(left, right, (((0,), (0,)), ((), ())), preferred_element_...  9.59 us
    dot_general x5, matrix products, matmul(): return jnp.dot(left, right, preferred_element_type=F32)  7.65 us
    all_to_all x1, waiting for transfers between devices, body(): lax.all_to_all(both.transpose(2, 0, 1, 3).reshape(shares2, seeds, -1), ('...  7.23 us
    dot_general x2, matrix products, inner_cols(): lax.dot_general(left, right, (((1,), (1,)), ((), ())), preferred_element_...  5.36 us
  transfers between devices with their start and end apart: 6, of which 2 were waited for; matrix products, arithmetic and copies ran while one was open for 20% of the time, Pallas kernels for 39%

profile of v2, /device:TPU:0, one launch (start us, length us, event | category | flops | bytes accessed | tf_op | source)
XLA Modules:
  0.0 179.7 jit_solution(12838198804054249596)
XLA Ops:
  7.2 5.3 %copy.22 = bf16[256,8,8,128]{3,2,1,0:T(8,128)(2,1)} copy(bf16[256,8,8,128]{3,1,2,0:T(8,128)(2,1)} %bitcast.71) | data formatting | bytes 8388608
  12.7 0.7 all-gather.8.cloned.1.call-update
  13.4 0.6 all_to_all.12
  14.0 5.2 %all-to-all-start = ((s32[4,1,256]{2,1,0:T(1,128)}), s32[4,1,256]{2,1,0:T(1,128)S(1)}, u32[]{:S(2)}, u32[]{:S(2)}) async-start(s32[4,1,256]{2,1,0:T(1,128)} %all_to_all.12), calls=%async_computation | async-start | bytes 8192 | tf_op jit(solution)/shard_map/all_to_all | solution.py:251
  19.1 5.5 %copy.23 = bf16[256,8,8,128]{3,2,1,0:T(8,128)(2,1)} copy(bf16[256,8,8,128]{3,1,2,0:T(8,128)(2,1)} %bitcast.72) | data formatting | bytes 8388608
  24.7 2.9 %copy-done.2 = bf16[256,8,8,128]{3,2,1,0:T(8,128)(2,1)S(1)} copy-done((bf16[256,8,8,128]{3,2,1,0:T(8,128)(2,1)S(1)}, bf16[256,8,8,128]{3,2,1,0:T(8,128)(2,1)}, u32[]{:S(2)}) %copy-start.2) | copy-done | bytes 4194328
  27.6 2.0 %pick_rows.1 = bf16[1024,8,128]{2,1,0:T(8,128)(2,1)S(1)} custom-call(s32[1024]{0:T(1024)S(1)} %bitcast.68, bf16[2048,8,128]{2,1,0:T(8,128)(2,1)S(1)} %bitcast.56), custom_call_target="tpu_custom_call" | custom-call | bytes 25165824 | tf_op jit(solution)/shard_map/pick_rows/pallas_call | solution.py:47
  29.6 1.3 copy-done.4
  30.9 4.6 %all-to-all-start.1 = ((bf16[4,256,8,128]{3,2,1,0:T(8,128)(2,1)}), bf16[4,256,8,128]{3,2,1,0:T(8,128)(2,1)}, u32[]{:S(2)}, u32[]{:S(2)}) async-start(bf16[4,256,8,128]{3,2,1,0:T(8,128)(2,1)} %bitcast.57), calls=%async_computation.1 | async-start | bytes 4194304 | tf_op jit(solution)/shard_map/all_to_all | solution.py:256
  35.5 0.7 reduce.1.hop2_ref
  36.2 2.4 %convolution_multiply_fusion = bf16[64,1024]{1,0:T(8,128)(2,1)S(1)} fusion(bf16[64,1024]{1,0:T(8,128)(2,1)S(1)} %copy-done.13, bf16[1024,1024]{1,0:T(8,128)(2,1)} %param.21), kind=kOutput, calls=%fused_computation.11 | convolution fusion | flops 134348800 | bytes 2359296 | tf_op jit(solution)/shard_map/dot_general | solution.py:18
  38.6 1.7 broadcast_in_dim.3
  40.2 3.6 %reshape.73 = bf16[640,1024]{1,0:T(8,128)(2,1)} reshape(bf16[64,10,1024]{2,1,0:T(8,128)(2,1)} %broadcast_in_dim.3) | data formatting | bytes 2621440 | tf_op jit(solution)/shard_map/reshape | solution.py:276
  43.9 0.6 fusion.23
  44.4 3.0 %fusion.30 = bf16[64,1024]{1,0:T(8,128)(2,1)} fusion(bf16[64,1024]{1,0:T(8,128)(2,1)S(1)} %copy-done.13, bf16[1024,1024]{1,0:T(8,128)(2,1)} %param.20), kind=kOutput, calls=%fused_computation.42 | convolution fusion | flops 134217728 | bytes 2359296 | tf_op jit(solution)/shard_map/dot_general | solution.py:18
  47.5 13.8 %all-to-all-done.1 = bf16[4,256,8,128]{3,2,1,0:T(8,128)(2,1)} async-done(((bf16[4,256,8,128]{3,2,1,0:T(8,128)(2,1)}), bf16[4,256,8,128]{3,2,1,0:T(8,128)(2,1)}, u32[]{:S(2)}, u32[]{:S(2)}) %all-to-all-start.1) | async-done | bytes 2097184 | tf_op jit(solution)/shard_map/all_to_all | solution.py:256
  61.3 3.4 %copy-done.3 = bf16[4096,8,128]{2,1,0:T(8,128)(2,1)S(1)} copy-done((bf16[4096,8,128]{2,1,0:T(8,128)(2,1)S(1)}, bf16[4096,8,128]{2,1,0:T(8,128)(2,1)}, u32[]{:S(2)}) %copy-start.3) | copy-done | bytes 8388632
  64.7 0.8 copy-done.7
  65.5 17.9 %gather_tree.1 = (bf16[704,8,128]{2,1,0:T(8,128)(2,1)S(1)}, bf16[704,8,128]{2,1,0:T(8,128)(2,1)S(1)}) custom-call(s32[64]{0:T(128)S(1)} %bitcast.69, s32[640]{0:T(1024)S(1)} %reduce.hop1_ref, s32[9600]{0:T(1024)S(1)} %copy-done.7, bf16[4096,8,128]{2,1,0:T(8,128)(2,1)S(1)} %copy-done.3, bf16[1024,8,128]{2,1,0:T(8,128)(2,1)} %bitcast.3.cold_ref), custom_call_target="tpu_custom_call" | custom-call | bytes 83886080 | tf_op jit(solution)/shard_map/gather_tree/pallas_call | solution.py:102
  83.5 1.7 fusion.28
  85.2 0.1 copy-done.12
  85.3 3.0 %fusion = (bf16[704,1024]{1,0:T(8,128)(2,1)}, bf16[704,1024]{1,0:T(8,128)(2,1)S(1)}) fusion(bf16[640,1024]{1,0:T(8,128)(2,1)S(1)} %copy-done.12, bf16[64,1024]{1,0:T(8,128)(2,1)S(1)} %copy-done.17, f32[704,1024]{1,0:T(8,128)S(1)} %fusion.28, bf16[1024,1024]{1,0:T(8,128)(2,1)S(1)} %copy-done, bf16[88,8,8,128]{3,2,1,0:T(8,128)(2,1)S(1)} %bitcast.62), kind=kOutput, calls=%fused_computation.1 | convolution fusion | flops 1482883072 | bytes 10747904 | tf_op jit(solution)/shard_map/dot_general | solution.py:22
  88.3 0.3 fusion.7
  88.7 0.7 copy-done.15
  89.4 0.2 copy.20
  89.6 0.2 copy.19
  89.9 1.3 maximum_bitcast_fusion
  91.2 1.8 %reshape.78 = bf16[8,64,256]{2,1,0:T(8,128)(2,1)} reshape(bf16[8,64,2,128]{3,2,1,0:T(2,128)(2,1)} %maximum_bitcast_fusion) | data formatting | bytes 524288 | tf_op jit(solution)/shard_map/reshape | solution.py:285
  93.0 3.4 %all-to-all-start.2 = ((bf16[8,64,256]{2,1,0:T(8,128)(2,1)}), bf16[8,64,256]{2,1,0:T(8,128)(2,1)S(1)}, u32[]{:S(2)}, u32[]{:S(2)}) async-start(bf16[8,64,256]{2,1,0:T(8,128)(2,1)} %reshape.78), calls=%async_computation.2 | async-start | bytes 524288 | tf_op jit(solution)/shard_map/all_to_all | solution.py:284
  96.4 0.2 all-gather.6.cloned.1.call-start
  96.7 1.5 copy.34
  98.2 7.2 %all-to-all-done.2 = bf16[8,64,256]{2,1,0:T(8,128)(2,1)S(1)} async-done(((bf16[8,64,256]{2,1,0:T(8,128)(2,1)}), bf16[8,64,256]{2,1,0:T(8,128)(2,1)S(1)}, u32[]{:S(2)}, u32[]{:S(2)}) %all-to-all-start.2) | async-done | bytes 262176 | tf_op jit(solution)/shard_map/all_to_all | solution.py:284
  105.4 0.7 copy-done.14
  106.1 2.6 %convolution_convert_fusion = bf16[512,1024]{1,0:T(8,128)(2,1)S(1)} fusion(bf16[704,1024]{1,0:T(8,128)(2,1)} %get-tuple-element.13, bf16[704,1024]{1,0:T(8,128)(2,1)} %bitcast.73, s32[]{:T(128)S(6)} %select_n.20), kind=kOutput, calls=%fused_computation.4 | convolution fusion | flops 738721792 | bytes 3211268 | tf_op jit(solution)/shard_map/dot_general | solution.py:14
  108.7 0.4 copy.35
  109.1 1.0 copy-done.24
  110.1 1.0 convolution_convert_fusion.1
  111.1 0.5 copy-done.11
  111.6 1.0 fusion.12
  112.6 1.0 fusion.14
  113.7 50.1 %reduce_pair.1 = (f32[4,32,1024]{2,1,0:T(8,128)S(1)}, f32[4,32,1024]{2,1,0:T(8,128)S(1)}) custom-call(f32[4,4,32,1024]{3,2,1,0:T(8,128)S(1)} %bitcast.59, f32[4,4,32,1024]{3,2,1,0:T(8,128)S(1)} %bitcast.58, bf16[4,4,32,1024]{3,2,1,0:T(8,128)(2,1)S(1)} %bitcast.65, bf16[4,4,32,1024]{3,2,1,0:T(8,128)(2,1)S(1)} %bitcast.64), custom_call_target="tpu_custom_call" | custom-call | bytes 104857600 | tf_op jit(solution)/shard_map/reduce_pair/pallas_call | solution.py:202
  163.8 1.5 fusion.16
  165.3 0.1 copy-done.9
  165.4 1.1 fusion.6
  166.6 3.9 %fusion.31 = f32[256,1024]{1,0:T(8,128)S(1)} fusion(bf16[2048,256]{1,0:T(8,128)(2,1)} %bitcast.81, bf16[2048,1024]{1,0:T(8,128)(2,1)} %all-gather.8.cloned.1.call-done), kind=kOutput, calls=%fused_computation.43 | convolution fusion | flops 1073741824 | bytes 6291456 | tf_op jit(solution)/shard_map/dot_general | solution.py:14
  170.5 1.1 fusion.29
  171.6 0.8 copy.38
  172.4 0.8 copy.39
  (53 shorter events, 0.3 us)
Async XLA Ops:
  7.2 78.0 %copy-start = (bf16[1024,1024]{1,0:T(8,128)(2,1)S(1)}, bf16[1024,1024]{1,0:T(8,128)(2,1)}, u32[]{:S(2)}) copy-start(bf16[1024,1024]{1,0:T(8,128)(2,1)} %param.19) | copy-start | bytes 6291460
  7.2 54.1 %all-gather.4.cloned.1.call-start = ((), (), s32[]{:S(2)}) async-start(), calls=%async_computation.3 | async-start | bytes 12582912 | tf_op jit(solution)/shard_map/all_gather | solution.py:253
  12.6 0.8 copy-start.20
  12.6 154.0 %all-gather.8.cloned.1.call-start = ((), (), s32[]{:S(2)}) async-start(), calls=%async_computation.5 | async-start | bytes 4325376 | tf_op jit(solution)/shard_map/all_gather | solution.py:257
  14.0 10.7 %all-to-all-start = ((s32[4,1,256]{2,1,0:T(1,128)}), s32[4,1,256]{2,1,0:T(1,128)S(1)}, u32[]{:S(2)}, u32[]{:S(2)}) async-start(s32[4,1,256]{2,1,0:T(1,128)} %all_to_all.12), calls=%async_computation | async-start | bytes 8192 | tf_op jit(solution)/shard_map/all_to_all | solution.py:251
  24.7 2.9 %copy-start.2 = (bf16[256,8,8,128]{3,2,1,0:T(8,128)(2,1)S(1)}, bf16[256,8,8,128]{3,2,1,0:T(8,128)(2,1)}, u32[]{:S(2)}) copy-start(bf16[256,8,8,128]{3,2,1,0:T(8,128)(2,1)} %copy.23) | copy-start | bytes 12582916
  29.6 1.3 copy-start.4
  30.9 4.6 %copy-start.19 = (s32[1,9600]{1,0:T(1,128)S(1)}, s32[1,9600]{1,0:T(1,128)}, u32[]{:S(2)}) copy-start(s32[1,9600]{1,0:T(1,128)} %param.15) | copy-start | bytes 115204
  30.9 5.3 %copy-start.21 = (s32[1,640]{1,0:T(1,128)S(1)}, s32[1,640]{1,0:T(1,128)}, u32[]{:S(2)}) copy-start(s32[1,640]{1,0:T(1,128)} %param.14) | copy-start | bytes 7684
  30.9 5.3 %copy-start.13 = (bf16[64,1024]{1,0:T(8,128)(2,1)S(1)}, bf16[64,1024]{1,0:T(8,128)(2,1)}, u32[]{:S(2)}) copy-start(bf16[64,1024]{1,0:T(8,128)(2,1)} %param.17) | copy-start | bytes 393220
  30.9 30.4 %all-to-all-start.1 = ((bf16[4,256,8,128]{3,2,1,0:T(8,128)(2,1)}), bf16[4,256,8,128]{3,2,1,0:T(8,128)(2,1)}, u32[]{:S(2)}, u32[]{:S(2)}) async-start(bf16[4,256,8,128]{3,2,1,0:T(8,128)(2,1)} %bitcast.57), calls=%async_computation.1 | async-start | bytes 4194304 | tf_op jit(solution)/shard_map/all_to_all | solution.py:256
  40.2 21.1 %copy-start.8 = (s32[1,64]{1,0:T(1,128)S(1)}, s32[1,64]{1,0:T(1,128)}, u32[]{:S(2)}) copy-start(s32[1,64]{1,0:T(1,128)} %param.13) | copy-start | bytes 772
  61.3 3.4 %copy-start.3 = (bf16[4096,8,128]{2,1,0:T(8,128)(2,1)S(1)}, bf16[4096,8,128]{2,1,0:T(8,128)(2,1)}, u32[]{:S(2)}) copy-start(bf16[4096,8,128]{2,1,0:T(8,128)(2,1)} %all-gather.4.cloned.1.call-done.hot_ref) | copy-start | bytes 25165828
  64.7 0.8 copy-start.7
  65.5 18.0 %copy-start.22 = (bf16[1024,1024]{1,0:T(8,128)(2,1)S(1)}, bf16[1024,1024]{1,0:T(8,128)(2,1)}, u32[]{:S(2)}) copy-start(bf16[1024,1024]{1,0:T(8,128)(2,1)} %param.18) | copy-start | bytes 6291460
  83.4 1.7 copy-start.5
  83.4 1.8 %copy-start.12 = (bf16[640,1024]{1,0:T(8,128)(2,1)S(1)}, bf16[640,1024]{1,0:T(8,128)(2,1)}, u32[]{:S(2)}) copy-start(bf16[640,1024]{1,0:T(8,128)(2,1)} %reshape.73) | copy-start | bytes 3932164
  83.5 1.8 %copy-start.17 = (bf16[64,1024]{1,0:T(8,128)(2,1)S(1)}, bf16[64,1024]{1,0:T(8,128)(2,1)}, u32[]{:S(2)}) copy-start(bf16[64,1024]{1,0:T(8,128)(2,1)} %fusion.30) | copy-start | bytes 393220
  85.3 3.0 %copy-start.23 = (pred[640]{0:T(1024)(128)(4,1)S(1)}, pred[640]{0:T(1024)(128)(4,1)}, u32[]{:S(2)}) copy-start(pred[640]{0:T(1024)(128)(4,1)} %fusion.23) | copy-start | bytes 1924
  88.3 1.6 copy-start.18
  88.6 0.8 copy-start.15
  88.6 8.0 %copy-start.6 = (bf16[704,8,128]{2,1,0:T(8,128)(2,1)S(1)}, bf16[704,8,128]{2,1,0:T(8,128)(2,1)}, u32[]{:S(2)}) copy-start(bf16[704,8,128]{2,1,0:T(8,128)(2,1)} %copy-done.5) | copy-start | bytes 4325380
  93.0 12.4 %all-to-all-start.2 = ((bf16[8,64,256]{2,1,0:T(8,128)(2,1)}), bf16[8,64,256]{2,1,0:T(8,128)(2,1)S(1)}, u32[]{:S(2)}, u32[]{:S(2)}) async-start(bf16[8,64,256]{2,1,0:T(8,128)(2,1)} %reshape.78), calls=%async_computation.2 | async-start | bytes 524288 | tf_op jit(solution)/shard_map/all_to_all | solution.py:284
  96.4 70.2 %all-gather.6.cloned.1.call-start = ((), (), s32[]{:S(2)}) async-start(), calls=%async_computation.4 | async-start | bytes 1310720 | tf_op jit(solution)/shard_map/all_gather | solution.py:288
  105.4 0.7 copy-start.14
  108.7 1.4 copy-start.24
  110.1 1.5 copy-start.11
  113.7 50.1 %copy-start.10 = (bf16[1024,1024]{1,0:T(8,128)(2,1)S(1)}, bf16[1024,1024]{1,0:T(8,128)(2,1)}, u32[]{:S(2)}) copy-start(bf16[1024,1024]{1,0:T(8,128)(2,1)} %param.20) | copy-start | bytes 6291460
  163.8 1.7 copy-start.9
  163.8 1.6 copy-start.16
  166.6 6.6 %copy-start.1 = (bf16[1024,1024]{1,0:T(8,128)(2,1)S(1)}, bf16[1024,1024]{1,0:T(8,128)(2,1)}, u32[]{:S(2)}) copy-start(bf16[1024,1024]{1,0:T(8,128)(2,1)} %param.19) | copy-start | bytes 6291460
Sparse Core Ops, SparseCore 0:
  12.7 22.5 all-gather.3
  38.3 74.0 all-gather.7
  114.5 40.7 all-gather.5

commit v3 on v2

--- a/solution.py
+++ b/solution.py
@@ -249,8 +249,8 @@
     tile = (width // LANES, LANES)
 
     asked = lax.all_to_all(cold_ask[0], "hst", split_axis=0, concat_axis=0, tiled=True)
-    hot_tiles = hot_table.reshape((hot_table.shape[0],) + tile)
-    hot_full = lax.all_gather(hot_tiles, "clique", axis=0, tiled=True)
+    hot_full = lax.all_gather(hot_table, "clique", axis=0, tiled=True)
+    hot_full = hot_full.reshape((hot_full.shape[0],) + tile)
     cold_tiles = cold_table.reshape((cold_table.shape[0],) + tile)
     picked = pick_rows(asked.reshape(-1), cold_tiles).reshape((owners, cap) + tile)
     cold_rows = lax.all_to_all(picked, "hst", split_axis=0, concat_axis=0, tiled=True)

time: 181 us -> 176 us (0.972)
  waiting for transfers between devices: 21.8 us -> 13.4 us
  local copies, waits for them, and re-layouts: 35.2 us -> 38.8 us
    all_to_all x1, waiting for transfers between devices: 13.8 us -> 4.87 us  [body(): lax.all_to_all(picked, 'hst', split_axis=0, concat_axis=0, tiled=True)]
    unnamed x59, local copies, waits for them, and re-layouts: 26 us -> 29.5 us
  transfers between devices with their start and end apart: 6 -> 6, of which waited for: 2 -> 2; matrix products, arithmetic and copies ran while one was open for 20% -> 26% of each run, Pallas kernels for 39% -> 40%
where the time goes in v3:
time: 176 us; the launch traced here: 175 us
  Pallas kernels  70.1 us (40%)
  local copies, waits for them, and re-layouts  38.8 us (22%)
  matrix products  22.6 us (13%)
  between operations  14.1 us (8%)
  starting transfers between devices  13.5 us (8%)
  waiting for transfers between devices  13.4 us (8%)
  other arithmetic  2.6 us (1%)
    pallas_call x1, Pallas kernels, reduce_pair(): pl.pallas_call(reduce_kernel, out_shape=(out, out), in_specs=[pl.BlockSpe...  50.1 us
    unnamed x59, local copies, waits for them, and re-layouts  29.5 us
    pallas_call x1, Pallas kernels, gather_tree(): pl.pallas_call(tree_kernel, out_shape=(out, out), in_specs=[pl.BlockSpec(...  17.9 us
    dot_general x5, matrix products, inner_rows(): lax.dot_general(left, right, (((0,), (0,)), ((), ())), preferred_element_...  9.59 us
    dot_general x5, matrix products, matmul(): return jnp.dot(left, right, preferred_element_type=F32)  7.65 us
    all_to_all x1, waiting for transfers between devices, body(): lax.all_to_all(both.transpose(2, 0, 1, 3).reshape(shares2, seeds, -1), ('...  7.14 us
    dot_general x2, matrix products, inner_cols(): lax.dot_general(left, right, (((1,), (1,)), ((), ())), preferred_element_...  5.36 us
    all_to_all x1, starting transfers between devices, body(): lax.all_to_all(cold_ask[0], 'hst', split_axis=0, concat_axis=0, tiled=True)  5.16 us
  transfers between devices with their start and end apart: 6, of which 2 were waited for; matrix products, arithmetic and copies ran while one was open for 26% of the time, Pallas kernels for 40%

profile of v3, /device:TPU:0, one launch (start us, length us, event | category | flops | bytes accessed | tf_op | source)
XLA Modules:
  0.0 174.9 jit_solution(6162070718377517119)
XLA Ops:
  7.2 0.7 all-gather.4.cloned.1.call-update
  8.0 0.7 all-gather.8.cloned.1.call-update
  8.7 0.6 all_to_all.12
  9.3 5.2 %all-to-all-start = ((s32[4,1,256]{2,1,0:T(1,128)}), s32[4,1,256]{2,1,0:T(1,128)S(1)}, u32[]{:S(2)}, u32[]{:S(2)}) async-start(s32[4,1,256]{2,1,0:T(1,128)} %all_to_all.12), calls=%async_computation | async-start | bytes 8192 | tf_op jit(solution)/shard_map/all_to_all | solution.py:251
  14.4 5.4 %copy.23 = bf16[256,8,8,128]{3,2,1,0:T(8,128)(2,1)} copy(bf16[256,8,8,128]{3,1,2,0:T(8,128)(2,1)} %bitcast.72) | data formatting | bytes 8388608
  19.9 2.9 %copy-done.3 = bf16[256,8,8,128]{3,2,1,0:T(8,128)(2,1)S(1)} copy-done((bf16[256,8,8,128]{3,2,1,0:T(8,128)(2,1)S(1)}, bf16[256,8,8,128]{3,2,1,0:T(8,128)(2,1)}, u32[]{:S(2)}) %copy-start.3) | copy-done | bytes 4194328
  22.8 2.0 %pick_rows.1 = bf16[1024,8,128]{2,1,0:T(8,128)(2,1)S(1)} custom-call(s32[1024]{0:T(1024)S(1)} %bitcast.69, bf16[2048,8,128]{2,1,0:T(8,128)(2,1)S(1)} %bitcast.57), custom_call_target="tpu_custom_call" | custom-call | bytes 25165824 | tf_op jit(solution)/shard_map/pick_rows/pallas_call | solution.py:47
  24.8 1.4 copy-done.4
  26.2 4.6 %all-to-all-start.1 = ((bf16[4,256,8,128]{3,2,1,0:T(8,128)(2,1)}), bf16[4,256,8,128]{3,2,1,0:T(8,128)(2,1)}, u32[]{:S(2)}, u32[]{:S(2)}) async-start(bf16[4,256,8,128]{3,2,1,0:T(8,128)(2,1)} %bitcast.58), calls=%async_computation.1 | async-start | bytes 4194304 | tf_op jit(solution)/shard_map/all_to_all | solution.py:256
  30.8 0.7 reduce.1.hop2_ref
  31.5 2.4 %convolution_multiply_fusion = bf16[64,1024]{1,0:T(8,128)(2,1)S(1)} fusion(bf16[64,1024]{1,0:T(8,128)(2,1)S(1)} %copy-done.13, bf16[1024,1024]{1,0:T(8,128)(2,1)} %param.21), kind=kOutput, calls=%fused_computation.11 | convolution fusion | flops 134348800 | bytes 2359296 | tf_op jit(solution)/shard_map/dot_general | solution.py:18
  33.9 1.7 broadcast_in_dim.3
  35.5 3.7 %reshape.73 = bf16[640,1024]{1,0:T(8,128)(2,1)} reshape(bf16[64,10,1024]{2,1,0:T(8,128)(2,1)} %broadcast_in_dim.3) | data formatting | bytes 2621440 | tf_op jit(solution)/shard_map/reshape | solution.py:276
  39.2 0.6 fusion.23
  39.8 3.0 %fusion.30 = bf16[64,1024]{1,0:T(8,128)(2,1)} fusion(bf16[64,1024]{1,0:T(8,128)(2,1)S(1)} %copy-done.13, bf16[1024,1024]{1,0:T(8,128)(2,1)} %param.20), kind=kOutput, calls=%fused_computation.42 | convolution fusion | flops 134217728 | bytes 2359296 | tf_op jit(solution)/shard_map/dot_general | solution.py:18
  42.8 8.9 %copy.22 = bf16[512,8,8,128]{3,2,1,0:T(8,128)(2,1)} copy(bf16[512,8,8,128]{3,1,2,0:T(8,128)(2,1)} %bitcast.71) | data formatting | bytes 16777216
  51.7 4.9 %all-to-all-done.1 = bf16[4,256,8,128]{3,2,1,0:T(8,128)(2,1)} async-done(((bf16[4,256,8,128]{3,2,1,0:T(8,128)(2,1)}), bf16[4,256,8,128]{3,2,1,0:T(8,128)(2,1)}, u32[]{:S(2)}, u32[]{:S(2)}) %all-to-all-start.1) | async-done | bytes 2097184 | tf_op jit(solution)/shard_map/all_to_all | solution.py:256
  56.6 3.4 %copy-done.2 = bf16[512,8,8,128]{3,2,1,0:T(8,128)(2,1)S(1)} copy-done((bf16[512,8,8,128]{3,2,1,0:T(8,128)(2,1)S(1)}, bf16[512,8,8,128]{3,2,1,0:T(8,128)(2,1)}, u32[]{:S(2)}) %copy-start.2) | copy-done | bytes 8388632
  60.0 0.8 copy-done.7
  60.8 17.9 %gather_tree.1 = (bf16[704,8,128]{2,1,0:T(8,128)(2,1)S(1)}, bf16[704,8,128]{2,1,0:T(8,128)(2,1)S(1)}) custom-call(s32[64]{0:T(128)S(1)} %bitcast.70, s32[640]{0:T(1024)S(1)} %reduce.hop1_ref, s32[9600]{0:T(1024)S(1)} %copy-done.7, bf16[4096,8,128]{2,1,0:T(8,128)(2,1)S(1)} %bitcast.56, bf16[1024,8,128]{2,1,0:T(8,128)(2,1)} %bitcast.3.cold_ref), custom_call_target="tpu_custom_call" | custom-call | bytes 83886080 | tf_op jit(solution)/shard_map/gather_tree/pallas_call | solution.py:102
  78.8 1.7 fusion.28
  80.4 0.1 copy-done.12
  80.6 3.0 %fusion = (bf16[704,1024]{1,0:T(8,128)(2,1)}, bf16[704,1024]{1,0:T(8,128)(2,1)S(1)}) fusion(bf16[640,1024]{1,0:T(8,128)(2,1)S(1)} %copy-done.12, bf16[64,1024]{1,0:T(8,128)(2,1)S(1)} %copy-done.17, f32[704,1024]{1,0:T(8,128)S(1)} %fusion.28, bf16[1024,1024]{1,0:T(8,128)(2,1)S(1)} %copy-done, bf16[88,8,8,128]{3,2,1,0:T(8,128)(2,1)S(1)} %bitcast.63), kind=kOutput, calls=%fused_computation.1 | convolution fusion | flops 1482883072 | bytes 10747904 | tf_op jit(solution)/shard_map/dot_general | solution.py:22
  83.6 0.3 fusion.7
  84.0 0.7 copy-done.15
  84.7 0.2 copy.20
  84.9 0.2 copy.19
  85.2 1.3 maximum_bitcast_fusion
  86.5 1.8 %reshape.78 = bf16[8,64,256]{2,1,0:T(8,128)(2,1)} reshape(bf16[8,64,2,128]{3,2,1,0:T(2,128)(2,1)} %maximum_bitcast_fusion) | data formatting | bytes 524288 | tf_op jit(solution)/shard_map/reshape | solution.py:285
  88.3 3.4 %all-to-all-start.2 = ((bf16[8,64,256]{2,1,0:T(8,128)(2,1)}), bf16[8,64,256]{2,1,0:T(8,128)(2,1)S(1)}, u32[]{:S(2)}, u32[]{:S(2)}) async-start(bf16[8,64,256]{2,1,0:T(8,128)(2,1)} %reshape.78), calls=%async_computation.2 | async-start | bytes 524288 | tf_op jit(solution)/shard_map/all_to_all | solution.py:284
  91.7 0.2 all-gather.6.cloned.1.call-start
  91.9 1.5 copy.34
  93.5 7.1 %all-to-all-done.2 = bf16[8,64,256]{2,1,0:T(8,128)(2,1)S(1)} async-done(((bf16[8,64,256]{2,1,0:T(8,128)(2,1)}), bf16[8,64,256]{2,1,0:T(8,128)(2,1)S(1)}, u32[]{:S(2)}, u32[]{:S(2)}) %all-to-all-start.2) | async-done | bytes 262176 | tf_op jit(solution)/shard_map/all_to_all | solution.py:284
  100.6 0.7 copy-done.14
  101.3 2.6 %convolution_convert_fusion = bf16[512,1024]{1,0:T(8,128)(2,1)S(1)} fusion(bf16[704,1024]{1,0:T(8,128)(2,1)} %get-tuple-element.13, bf16[704,1024]{1,0:T(8,128)(2,1)} %bitcast.73, s32[]{:T(128)S(6)} %select_n.20), kind=kOutput, calls=%fused_computation.4 | convolution fusion | flops 738721792 | bytes 3211268 | tf_op jit(solution)/shard_map/dot_general | solution.py:14
  103.9 0.4 copy.35
  104.3 1.0 copy-done.24
  105.3 1.0 convolution_convert_fusion.1
  106.3 0.5 copy-done.11
  106.8 1.0 fusion.12
  107.8 1.0 fusion.14
  108.9 50.1 %reduce_pair.1 = (f32[4,32,1024]{2,1,0:T(8,128)S(1)}, f32[4,32,1024]{2,1,0:T(8,128)S(1)}) custom-call(f32[4,4,32,1024]{3,2,1,0:T(8,128)S(1)} %bitcast.60, f32[4,4,32,1024]{3,2,1,0:T(8,128)S(1)} %bitcast.59, bf16[4,4,32,1024]{3,2,1,0:T(8,128)(2,1)S(1)} %bitcast.66, bf16[4,4,32,1024]{3,2,1,0:T(8,128)(2,1)S(1)} %bitcast.65), custom_call_target="tpu_custom_call" | custom-call | bytes 104857600 | tf_op jit(solution)/shard_map/reduce_pair/pallas_call | solution.py:202
  159.0 1.5 fusion.16
  160.6 1.1 fusion.6
  161.8 3.9 %fusion.31 = f32[256,1024]{1,0:T(8,128)S(1)} fusion(bf16[2048,256]{1,0:T(8,128)(2,1)} %bitcast.81, bf16[2048,1024]{1,0:T(8,128)(2,1)} %all-gather.8.cloned.1.call-done), kind=kOutput, calls=%fused_computation.43 | convolution fusion | flops 1073741824 | bytes 6291456 | tf_op jit(solution)/shard_map/dot_general | solution.py:14
  165.7 1.1 fusion.29
  166.8 0.8 copy.38
  167.6 0.8 copy.39
  (53 shorter events, 0.4 us)
Async XLA Ops:
  7.2 73.3 %copy-start = (bf16[1024,1024]{1,0:T(8,128)(2,1)S(1)}, bf16[1024,1024]{1,0:T(8,128)(2,1)}, u32[]{:S(2)}) copy-start(bf16[1024,1024]{1,0:T(8,128)(2,1)} %param.19) | copy-start | bytes 6291460
  7.2 1.5 copy-start.20
  7.2 35.6 %all-gather.4.cloned.1.call-start = ((), (), s32[]{:S(2)}) async-start(), calls=%async_computation.3 | async-start | bytes 12582912 | tf_op jit(solution)/shard_map/all_gather | solution.py:252
  7.9 153.9 %all-gather.8.cloned.1.call-start = ((), (), s32[]{:S(2)}) async-start(), calls=%async_computation.5 | async-start | bytes 4325376 | tf_op jit(solution)/shard_map/all_gather | solution.py:257
  9.3 10.6 %all-to-all-start = ((s32[4,1,256]{2,1,0:T(1,128)}), s32[4,1,256]{2,1,0:T(1,128)S(1)}, u32[]{:S(2)}, u32[]{:S(2)}) async-start(s32[4,1,256]{2,1,0:T(1,128)} %all_to_all.12), calls=%async_computation | async-start | bytes 8192 | tf_op jit(solution)/shard_map/all_to_all | solution.py:251
  19.9 2.9 %copy-start.3 = (bf16[256,8,8,128]{3,2,1,0:T(8,128)(2,1)S(1)}, bf16[256,8,8,128]{3,2,1,0:T(8,128)(2,1)}, u32[]{:S(2)}) copy-start(bf16[256,8,8,128]{3,2,1,0:T(8,128)(2,1)} %copy.23) | copy-start | bytes 12582916
  24.8 1.4 copy-start.4
  26.2 4.6 %copy-start.19 = (s32[1,9600]{1,0:T(1,128)S(1)}, s32[1,9600]{1,0:T(1,128)}, u32[]{:S(2)}) copy-start(s32[1,9600]{1,0:T(1,128)} %param.15) | copy-start | bytes 115204
  26.2 5.3 %copy-start.21 = (s32[1,640]{1,0:T(1,128)S(1)}, s32[1,640]{1,0:T(1,128)}, u32[]{:S(2)}) copy-start(s32[1,640]{1,0:T(1,128)} %param.14) | copy-start | bytes 7684
  26.2 5.3 %copy-start.13 = (bf16[64,1024]{1,0:T(8,128)(2,1)S(1)}, bf16[64,1024]{1,0:T(8,128)(2,1)}, u32[]{:S(2)}) copy-start(bf16[64,1024]{1,0:T(8,128)(2,1)} %param.17) | copy-start | bytes 393220
  26.2 30.4 %all-to-all-start.1 = ((bf16[4,256,8,128]{3,2,1,0:T(8,128)(2,1)}), bf16[4,256,8,128]{3,2,1,0:T(8,128)(2,1)}, u32[]{:S(2)}, u32[]{:S(2)}) async-start(bf16[4,256,8,128]{3,2,1,0:T(8,128)(2,1)} %bitcast.58), calls=%async_computation.1 | async-start | bytes 4194304 | tf_op jit(solution)/shard_map/all_to_all | solution.py:256
  42.8 13.8 %copy-start.8 = (s32[1,64]{1,0:T(1,128)S(1)}, s32[1,64]{1,0:T(1,128)}, u32[]{:S(2)}) copy-start(s32[1,64]{1,0:T(1,128)} %param.13) | copy-start | bytes 772
  56.6 3.4 %copy-start.2 = (bf16[512,8,8,128]{3,2,1,0:T(8,128)(2,1)S(1)}, bf16[512,8,8,128]{3,2,1,0:T(8,128)(2,1)}, u32[]{:S(2)}) copy-start(bf16[512,8,8,128]{3,2,1,0:T(8,128)(2,1)} %copy.22) | copy-start | bytes 25165828
  60.0 0.8 copy-start.7
  60.8 18.0 %copy-start.22 = (bf16[1024,1024]{1,0:T(8,128)(2,1)S(1)}, bf16[1024,1024]{1,0:T(8,128)(2,1)}, u32[]{:S(2)}) copy-start(bf16[1024,1024]{1,0:T(8,128)(2,1)} %param.18) | copy-start | bytes 6291460
  78.7 1.7 copy-start.5
  78.7 1.8 %copy-start.12 = (bf16[640,1024]{1,0:T(8,128)(2,1)S(1)}, bf16[640,1024]{1,0:T(8,128)(2,1)}, u32[]{:S(2)}) copy-start(bf16[640,1024]{1,0:T(8,128)(2,1)} %reshape.73) | copy-start | bytes 3932164
  78.7 1.8 %copy-start.17 = (bf16[64,1024]{1,0:T(8,128)(2,1)S(1)}, bf16[64,1024]{1,0:T(8,128)(2,1)}, u32[]{:S(2)}) copy-start(bf16[64,1024]{1,0:T(8,128)(2,1)} %fusion.30) | copy-start | bytes 393220
  80.6 3.0 %copy-start.23 = (pred[640]{0:T(1024)(128)(4,1)S(1)}, pred[640]{0:T(1024)(128)(4,1)}, u32[]{:S(2)}) copy-start(pred[640]{0:T(1024)(128)(4,1)} %fusion.23) | copy-start | bytes 1924
  83.5 1.6 copy-start.18
  83.9 0.8 copy-start.15
  83.9 8.0 %copy-start.6 = (bf16[704,8,128]{2,1,0:T(8,128)(2,1)S(1)}, bf16[704,8,128]{2,1,0:T(8,128)(2,1)}, u32[]{:S(2)}) copy-start(bf16[704,8,128]{2,1,0:T(8,128)(2,1)} %copy-done.5) | copy-start | bytes 4325380
  88.3 12.3 %all-to-all-start.2 = ((bf16[8,64,256]{2,1,0:T(8,128)(2,1)}), bf16[8,64,256]{2,1,0:T(8,128)(2,1)S(1)}, u32[]{:S(2)}, u32[]{:S(2)}) async-start(bf16[8,64,256]{2,1,0:T(8,128)(2,1)} %reshape.78), calls=%async_computation.2 | async-start | bytes 524288 | tf_op jit(solution)/shard_map/all_to_all | solution.py:284
  91.7 70.1 %all-gather.6.cloned.1.call-start = ((), (), s32[]{:S(2)}) async-start(), calls=%async_computation.4 | async-start | bytes 1310720 | tf_op jit(solution)/shard_map/all_gather | solution.py:288
  100.6 0.7 copy-start.14
  103.9 1.4 copy-start.24
  105.3 1.5 copy-start.11
  108.8 50.2 %copy-start.10 = (bf16[1024,1024]{1,0:T(8,128)(2,1)S(1)}, bf16[1024,1024]{1,0:T(8,128)(2,1)}, u32[]{:S(2)}) copy-start(bf16[1024,1024]{1,0:T(8,128)(2,1)} %param.20) | copy-start | bytes 6291460
  159.0 1.7 copy-start.9
  159.0 1.6 copy-start.16
  161.8 6.6 %copy-start.1 = (bf16[1024,1024]{1,0:T(8,128)(2,1)S(1)}, bf16[1024,1024]{1,0:T(8,128)(2,1)}, u32[]{:S(2)}) copy-start(bf16[1024,1024]{1,0:T(8,128)(2,1)} %param.19) | copy-start | bytes 6291460
Sparse Core Ops, SparseCore 0:
  9.6 22.5 all-gather.3
  35.1 72.3 all-gather.7
  109.6 40.8 all-gather.5
